TPU v7x, 128 devices: a whole 4x4x4 slice. The times are simulated.
128 devices in a mesh: section: 2 (over y_hi), ep: 16 (over y_lo, z, core), edp: 4 (over x).
Axes of the slice: x: 4, y: 4 (y_hi: 2, y_lo: 2; y = y_hi * 2 + y_lo), z: 4, core: 2. Of those that a mesh axis runs over, the one named last changes fastest.
Arguments:
- tokens: bfloat16 [2, 6144, 5120], P('section', 'ep', 'edp'), may hold values from -6 to 6
- out_grads: bfloat16 [2, 6144, 5120], P('section', 'ep', 'edp'), may hold values from -6 to 6
- gates: bfloat16 [2, 6144, 6], P('section', 'ep'), may hold values from 0.099609375 to 1.5
- routes: int32 [2, 6144, 6], P('section', 'ep'), may hold values from 0 to 159, as said below
- w_gate: bfloat16 [2, 16, 5120, 1536], P('section', 'ep', None, 'edp'), may hold values from -0.078125 to 0.078125
- w_up: bfloat16 [2, 16, 5120, 1536], P('section', 'ep', None, 'edp'), may hold values from -0.078125 to 0.078125
- w_down: bfloat16 [2, 16, 1536, 5120], P('section', 'ep', 'edp'), may hold values from -0.15625 to 0.15625
Outputs:
- grad_prev: bfloat16 [2, 6144, 5120], P('section', 'ep', 'edp')
- grad_w_gate: bfloat16 [2, 16, 5120, 1536], P('section', 'ep', None, 'edp')
- grad_w_up: bfloat16 [2, 16, 5120, 1536], P('section', 'ep', None, 'edp')
- grad_w_down: bfloat16 [2, 16, 1536, 5120], P('section', 'ep', 'edp')
Inputs may be any that keep to these rules, and one draw needn't show every extreme that they name: `routes`: each row names 6 different experts. Within one section, the rows of one index of ep name each window expert (an id that is a multiple of 10) at most 24 times; in every section some window expert is named exactly 24 times by the rows of every index of ep.
All inputs are finite; a program needn't handle non-finite values.
Results may differ from a plain program's by a relative error of at most 0.013.
Values may be sent and summed in bfloat16 or wider, within the bound.
No kernel may reach another device: no remote copies, remote signals or barrier semaphores. Data moves between devices by JAX's collectives and lax.ppermute only.
A program may use at most 128 MiB of HBM per device.

v0:
```python
import jax
import jax.numpy as jnp
from jax import lax
from jax.sharding import PartitionSpec as P

EXPERTS = 160
TOP = 6
CAP = 24


def passed_along(array, axis, by):
    length = lax.axis_size(axis)
    return lax.ppermute(array, axis, [(i, (i + by) % length) for i in range(length)])


def route_targets(block_routes, ep_count):
    group_size = EXPERTS // ep_count
    flat_routes = block_routes.reshape(-1)
    inside = flat_routes % group_size == 0
    expert_slot = flat_routes // group_size
    matches = (
        (expert_slot[:, None] == jnp.arange(ep_count, dtype=jnp.int32)[None, :]) & inside[:, None]
    ).astype(jnp.int32)
    earlier = jnp.cumsum(matches, axis=0) - matches
    position = jnp.sum(earlier * matches, axis=1)
    return jnp.where(inside, expert_slot * CAP + position, ep_count * CAP)


def slot_owners(targets, token_count, ep_count):
    token_index = jnp.arange(token_count * TOP, dtype=jnp.int32) // TOP
    empty_owner = jnp.full((ep_count * CAP,), token_count, jnp.int32)
    return empty_owner.at[targets].set(token_index, mode="drop")


def slot_gates(block_gates, targets, ep_count):
    empty_gate = jnp.zeros((ep_count * CAP,), block_gates.dtype)
    return empty_gate.at[targets].set(block_gates.reshape(-1), mode="drop")


def feature_join(pair):
    return (
        lax.all_gather(pair[0], "edp", axis=2, tiled=True),
        lax.all_gather(pair[1], "edp", axis=2, tiled=True),
    )


def feature_sum(terms):
    return lax.psum_scatter(
        terms.astype(jnp.bfloat16), "edp", scatter_dimension=2, tiled=True
    ).astype(jnp.float32)


def contract_hidden(left, right):
    return lax.dot_general(
        left, right, (((1,), (1,)), ((), ())), preferred_element_type=jnp.float32
    )


def contract_rows(left, right):
    return lax.dot_general(
        left, right, (((0,), (0,)), ((), ())), preferred_element_type=jnp.float32
    )


def body(tokens, out_grads, gates, routes, w_gate, w_up, w_down):
    ep_count = lax.axis_size("ep")
    token_count = tokens.shape[1]
    targets = route_targets(routes[0], ep_count)
    owners = slot_owners(targets, token_count, ep_count)
    source_x, source_dy = feature_join((tokens, out_grads))
    width = source_x.shape[2]
    send_x = jnp.take(source_x[0], owners, axis=0, mode="fill", fill_value=0).reshape(
        ep_count, CAP, width
    )
    send_dy = jnp.take(source_dy[0], owners, axis=0, mode="fill", fill_value=0).reshape(
        ep_count, CAP, width
    )
    send_gate = slot_gates(gates[0], targets, ep_count).reshape(ep_count, CAP)
    recv_x, recv_dy, recv_gate = (
        lax.all_to_all(send_x, "ep", split_axis=0, concat_axis=0, tiled=True),
        lax.all_to_all(send_dy, "ep", split_axis=0, concat_axis=0, tiled=True),
        lax.all_to_all(send_gate, "ep", split_axis=0, concat_axis=0, tiled=True),
    )
    row_count = ep_count * CAP
    model_width = recv_x.shape[2]
    rows_x = recv_x.reshape(row_count, model_width)
    rows_dy = recv_dy.reshape(row_count, model_width)
    weight = recv_gate.reshape(row_count).astype(jnp.float32)[:, None]
    gate_weight = w_gate[0, 0]
    up_weight = w_up[0, 0]
    down_weight = w_down[0, 0]
    gate_pre = jnp.dot(rows_x, gate_weight, preferred_element_type=jnp.float32)
    up_pre = jnp.dot(rows_x, up_weight, preferred_element_type=jnp.float32)
    back = contract_hidden(rows_dy, down_weight)
    sigmoid_gate = jax.nn.sigmoid(gate_pre)
    swish = gate_pre * sigmoid_gate
    hidden = swish * up_pre
    d_hidden = weight * back
    d_gate = (d_hidden * up_pre * sigmoid_gate * (1.0 + gate_pre * (1.0 - sigmoid_gate))).astype(
        jnp.bfloat16
    )
    d_up = (d_hidden * swish).astype(jnp.bfloat16)
    gated_hidden = (weight * hidden).astype(jnp.bfloat16)
    grad_gate = contract_rows(rows_x, d_gate).astype(jnp.bfloat16)
    grad_up = contract_rows(rows_x, d_up).astype(jnp.bfloat16)
    grad_down = contract_rows(gated_hidden, rows_dy).astype(jnp.bfloat16)
    partial_rows = contract_hidden(d_gate, gate_weight) + contract_hidden(d_up, up_weight)
    partial_rows = partial_rows.astype(jnp.bfloat16).reshape(ep_count, CAP, model_width)
    returned = lax.all_to_all(partial_rows, "ep", split_axis=0, concat_axis=0, tiled=True)
    slot_rows = feature_sum(returned.astype(jnp.float32)).astype(jnp.bfloat16)
    slot_rows = slot_rows.reshape(row_count, slot_rows.shape[2])
    chooser = (
        (
            targets.reshape(token_count, TOP)[:, :, None]
            == jnp.arange(row_count, dtype=jnp.int32)[None, None, :]
        )
        .any(axis=1)
        .astype(jnp.bfloat16)
    )
    input_grads = jnp.dot(chooser, slot_rows, preferred_element_type=jnp.float32).astype(
        jnp.bfloat16
    )
    grad_prev = passed_along(input_grads[None], "section", -1)
    return (grad_prev, grad_gate[None, None], grad_up[None, None], grad_down[None, None])


def solution(mesh):
    placed = (
        P("section", "ep", "edp"),
        P("section", "ep", "edp"),
        P("section", "ep", None),
        P("section", "ep", None),
        P("section", "ep", None, "edp"),
        P("section", "ep", None, "edp"),
        P("section", "ep", "edp", None),
    )
    return jax.shard_map(
        body,
        mesh=mesh,
        in_specs=placed,
        out_specs=(
            P("section", "ep", "edp"),
            P("section", "ep", None, "edp"),
            P("section", "ep", None, "edp"),
            P("section", "ep", "edp", None),
        ),
        check_vma=False,
    )
```

profile of v0, /device:TPU:1, one launch (start us, length us, event | category | flops | bytes accessed | tf_op | source)
XLA Modules:
  0.0 379.1 jit_solution(10063609343294243369)
XLA Ops:
  7.2 0.7 all-gather.3.cloned.1.call-update
  8.0 0.7 all-gather.5.cloned.1.call-update
  8.7 0.8 copy.24
  9.6 0.1 div.43
  9.7 0.1 div.42
  9.9 0.2 ne.105
  10.1 0.2 ne.103
  10.3 0.1 rem.65
  10.4 0.1 rem.63
  10.6 0.2 div.44
  10.7 0.2 ne.108
  10.9 0.2 rem.67
  11.2 4.6 %reduce-window.6 = s32[16,18,128]{2,1,0:T(8,128)S(1)} reduce-window(s32[16,18,128]{2,1,0:T(8,128)S(1)} %fusion.24, s32[]{:T(128)} %constant.28.clone.1), window={size=1x1x128 pad=0_0x0_0x127_0}, to_apply=%region_0.1 | reduce-window | flops 4681728 | bytes 294916 | tf_op jit(solution)/shard_map/reduce-window
  15.8 0.4 slice_reduce_fusion
  16.2 0.2 reduce-window.9
  16.4 0.2 copy.28
  16.6 0.2 reshape.245
  16.8 0.1 broadcast_add_fusion
  17.0 20.7 %scatter_custom_fusion = bf16[384]{0:T(512)(128)(2,1)S(1)} fusion(s32[2304]{0:T(1024)S(1)} %fusion.36, bf16[2304]{0:T(1024)(128)(2,1)S(1)} %reshape.245, bf16[]{:T(256)} %constant.51.clone.1), kind=kCustom, calls=%fused_computation.83 | custom fusion | bytes 770 | tf_op jit(solution)/shard_map/scatter | solution.py:37
  37.7 0.7 all_to_all.20
  38.4 7.8 %all-to-all-start = ((bf16[16,1,24]{2,1,0:T(2,128)(2,1)}), bf16[16,1,24]{2,1,0:T(2,128)(2,1)S(1)}, u32[]{:S(2)}, u32[]{:S(2)}) async-start(bf16[16,1,24]{2,1,0:T(2,128)(2,1)} %all_to_all.20), calls=%async_computation | async-start | bytes 16384 | tf_op jit(solution)/shard_map/all_to_all | solution.py:82
  46.3 9.1 %scatter_custom_fusion.1 = s32[384]{0:T(512)S(1)} fusion(s32[2304]{0:T(1024)S(1)} %fusion.36, s32[2304]{0:T(1024)S(1)} %add_select_fusion.2, s32[]{:T(128)} %constant.49.clone.1), kind=kCustom, calls=%fused_computation.81 | custom fusion | bytes 1540 | tf_op jit(solution)/shard_map/scatter | solution.py:32
  55.5 3.5 all-gather.3.cloned.1.call-done
  58.9 12.7 %gather_fusion = bf16[384,5120]{1,0:T(8,128)(2,1)} fusion(bf16[384,5120]{1,0:T(8,128)(2,1)} %bitcast.81, s32[1024]{0:T(1024)S(1)} %pad_clamp_fusion), kind=kCustom, calls=%fused_computation.clone | custom fusion | bytes 7865856 | tf_op jit(solution)/shard_map/jit(_take)/gather | solution.py:75
  71.6 35.4 %all-gather.5.cloned.1.call-done = bf16[1,384,5120]{2,1,0:T(8,128)(2,1)} async-done(((bf16[1,384,1280]{2,1,0:T(8,128)(2,1)}), bf16[1,384,5120]{2,1,0:T(8,128)(2,1)}) %all-gather.5.cloned.1.call-update) | async-done | bytes 3932176 | tf_op jit(solution)/shard_map/all_gather | solution.py:42
  107.0 12.7 %gather_fusion.1 = bf16[384,5120]{1,0:T(8,128)(2,1)} fusion(bf16[384,5120]{1,0:T(8,128)(2,1)} %bitcast.82, s32[1024]{0:T(1024)S(1)} %pad_clamp_fusion), kind=kCustom, calls=%fused_computation.1.clone | custom fusion | bytes 7865856 | tf_op jit(solution)/shard_map/jit(_take)/gather | solution.py:72
  119.6 5.7 %broadcast_select_fusion.1 = (bf16[384,5120]{1,0:T(8,128)(2,1)}, bf16[384,5120]{1,0:T(8,128)(2,1)}) fusion(bf16[384,5120]{1,0:T(8,128)(2,1)} %gather_fusion, pred[384]{0:T(512)(128)(4,1)S(1)} %compare_and_fusion, bf16[384,5120]{1,0:T(8,128)(2,1)} %gather_fusion.1), kind=kLoop, calls=%fused_computation.21 | loop fusion | flops 3932160 | bytes 15729024 | tf_op jit(solution)/shard_map/jit(_take)/select_n | solution.py:75
  125.3 52.7 %all_to_all.25 = bf16[16,24,5120]{2,1,0:T(8,128)(2,1)} all-to-all(bf16[16,24,5120]{2,1,0:T(8,128)(2,1)} %bitcast.84), channel_id=1, replica_groups=mesh['section'=2,'ep'=16,'edp'=4] {'ep'}, dimensions={0} | all-to-all | bytes 7864320 | tf_op jit(solution)/shard_map/all_to_all | solution.py:80
  178.0 5.2 %all-to-all-start.1 = ((bf16[16,24,5120]{2,1,0:T(8,128)(2,1)}), bf16[16,24,5120]{2,1,0:T(8,128)(2,1)}, u32[]{:S(2)}, u32[]{:S(2)}) async-start(bf16[16,24,5120]{2,1,0:T(8,128)(2,1)} %bitcast.83), calls=%async_computation.1 | async-start | bytes 7864320 | tf_op jit(solution)/shard_map/all_to_all | solution.py:81
  183.2 0.3 reduce-scatter.2.cloned.1.call-start
  183.6 5.6 %fusion.5 = f32[384,384]{1,0:T(8,128)S(1)} fusion(bf16[384,5120]{1,0:T(8,128)(2,1)} %bitcast.86, bf16[1,1,5120,384]{3,2,1,0:T(8,128)(2,1)} %param.13), kind=kOutput, calls=%fused_computation.13 | convolution fusion | flops 1509949440 | bytes 8454144 | tf_op jit(solution)/shard_map/dot_general | solution.py:92
  189.3 2.2 fusion.8
  191.5 42.5 %all-to-all-done.1 = bf16[16,24,5120]{2,1,0:T(8,128)(2,1)} async-done(((bf16[16,24,5120]{2,1,0:T(8,128)(2,1)}), bf16[16,24,5120]{2,1,0:T(8,128)(2,1)}, u32[]{:S(2)}, u32[]{:S(2)}) %all-to-all-start.1) | async-done | bytes 3932192 | tf_op jit(solution)/shard_map/all_to_all | solution.py:81
  234.0 5.8 %multiply_convert_fusion.1 = (bf16[384,384]{1,0:T(8,128)(2,1)S(1)}, bf16[384,384]{1,0:T(8,128)(2,1)S(1)}) fusion(f32[384,384]{1,0:T(8,128)S(1)} %fusion.5, f32[384,384]{1,0:T(8,128)S(1)} %fusion.8, bf16[384,5120]{1,0:T(8,128)(2,1)} %bitcast.6, bf16[1,1,384,5120]{3,2,1,0:T(8,128)(2,1)} %param.15, f32[384]{0:T(512)S(1)} %reshape.224), kind=kOutput, calls=%fused_computation.28 | convolution fusion | flops 1512013824 | bytes 9635328 | tf_op jit(solution)/shard_map/dot_general | solution.py:54
  239.8 2.2 fusion.3
  242.1 2.3 add_convert_fusion
  244.4 57.8 %all_to_all.26 = bf16[16,24,5120]{2,1,0:T(8,128)(2,1)} all-to-all(bf16[16,24,5120]{2,1,0:T(8,128)(2,1)S(1)} %bitcast.85), channel_id=1, replica_groups=mesh['section'=2,'ep'=16,'edp'=4] {'ep'}, dimensions={0} | all-to-all | bytes 7864320 | tf_op jit(solution)/shard_map/all_to_all | solution.py:109
  302.2 0.2 reduce_sum.14
  302.4 0.2 fusion.22
  302.7 0.7 fusion.12
  303.4 41.8 %reduce-scatter.2.cloned.1.call-done = bf16[16,24,1280]{2,1,0:T(8,128)(2,1)} async-done(((bf16[16,24,5120]{2,1,0:T(8,128)(2,1)}), bf16[16,24,1280]{2,1,0:T(8,128)(2,1)}) %reduce-scatter.2.cloned.1.call-update) | async-done | bytes 983056 | tf_op jit(solution)/shard_map/reduce_scatter | solution.py:48
  345.2 1.9 fusion.13
  347.1 3.1 collective-permute-start
  350.2 6.6 %fusion = bf16[1,1,5120,384]{3,2,1,0:T(8,128)(2,1)} fusion(bf16[384,5120]{1,0:T(8,128)(2,1)} %bitcast.87, bf16[384,384]{1,0:T(8,128)(2,1)S(1)} %get-tuple-element.6), kind=kOutput, calls=%fused_computation.8 | convolution fusion | flops 1511915520 | bytes 8159232 | tf_op jit(solution)/shard_map/dot_general | solution.py:60
  356.8 4.1 %fusion.1 = bf16[1,1,5120,384]{3,2,1,0:T(8,128)(2,1)} fusion(bf16[384,5120]{1,0:T(8,128)(2,1)S(1)} %bitcast.89, bf16[384,384]{1,0:T(8,128)(2,1)S(1)} %get-tuple-element.5), kind=kOutput, calls=%fused_computation.9 | convolution fusion | flops 1511915520 | bytes 8159232 | tf_op jit(solution)/shard_map/dot_general | solution.py:60
  361.0 6.4 %fusion.2 = bf16[1,1,384,5120]{3,2,1,0:T(8,128)(2,1)} fusion(bf16[384,5120]{1,0:T(8,128)(2,1)} %bitcast.6, f32[384,384]{1,0:T(8,128)S(1)} %fusion.8, f32[384]{0:T(512)S(1)} %reshape.224, f32[384,384]{1,0:T(8,128)S(1)} %fusion.5), kind=kOutput, calls=%fused_computation.10 | convolution fusion | flops 1512947712 | bytes 9045504 | tf_op jit(solution)/shard_map/dot_general | solution.py:60
  367.3 4.3 %collective-permute-done = bf16[1,384,1280]{2,1,0:T(8,128)(2,1)S(1)} collective-permute-done((bf16[1,384,1280]{2,1,0:T(8,128)(2,1)S(1)}, bf16[1,384,1280]{2,1,0:T(8,128)(2,1)S(1)}, u32[]{:S(2)}, u32[]{:S(2)}) %collective-permute-start) | collective-permute-done | bytes 983072 | tf_op jit(solution)/shard_map/ppermute | solution.py:13
  371.6 0.9 copy.33
  (32 shorter events, 0.7 us)
Async XLA Ops:
  7.2 9.2 %copy-start.5 = (bf16[1,384,6]{1,2,0:T(8,128)(2,1)S(1)}, bf16[1,384,6]{1,2,0:T(8,128)(2,1)}, u32[]{:S(2)}) copy-start(bf16[1,384,6]{1,2,0:T(8,128)(2,1)} %param.11) | copy-start | bytes 13828
  7.2 51.8 %all-gather.3.cloned.1.call-start = ((), (), s32[]{:S(2)}) async-start(), calls=%async_computation.5 | async-start | bytes 4915200 | tf_op jit(solution)/shard_map/all_gather | solution.py:43
  7.9 99.1 %all-gather.5.cloned.1.call-start = ((), (), s32[]{:S(2)}) async-start(), calls=%async_computation.6 | async-start | bytes 4915200 | tf_op jit(solution)/shard_map/all_gather | solution.py:42
  38.4 86.9 %all-to-all-start = ((bf16[16,1,24]{2,1,0:T(2,128)(2,1)}), bf16[16,1,24]{2,1,0:T(2,128)(2,1)S(1)}, u32[]{:S(2)}, u32[]{:S(2)}) async-start(bf16[16,1,24]{2,1,0:T(2,128)(2,1)} %all_to_all.20), calls=%async_computation | async-start | bytes 16384 | tf_op jit(solution)/shard_map/all_to_all | solution.py:82
  178.0 56.0 %all-to-all-start.1 = ((bf16[16,24,5120]{2,1,0:T(8,128)(2,1)}), bf16[16,24,5120]{2,1,0:T(8,128)(2,1)}, u32[]{:S(2)}, u32[]{:S(2)}) async-start(bf16[16,24,5120]{2,1,0:T(8,128)(2,1)} %bitcast.83), calls=%async_computation.1 | async-start | bytes 7864320 | tf_op jit(solution)/shard_map/all_to_all | solution.py:81
  183.2 162.0 %reduce-scatter.2.cloned.1.call-start = ((), (), s32[]{:S(2)}) async-start(), calls=%async_computation.7 | async-start | bytes 4915200 | tf_op jit(solution)/shard_map/reduce_scatter | solution.py:48
  183.6 5.7 %copy-start.1 = (bf16[16,24,5120]{2,1,0:T(8,128)(2,1)S(1)}, bf16[16,24,5120]{2,1,0:T(8,128)(2,1)}, u32[]{:S(2)}) copy-start(bf16[16,24,5120]{2,1,0:T(8,128)(2,1)} %all_to_all.25) | copy-start | bytes 11796484
  183.6 5.7 %copy-start.3 = (bf16[1,1,5120,384]{3,2,1,0:T(8,128)(2,1)S(1)}, bf16[1,1,5120,384]{3,2,1,0:T(8,128)(2,1)}, u32[]{:S(2)}) copy-start(bf16[1,1,5120,384]{3,2,1,0:T(8,128)(2,1)} %param.14) | copy-start | bytes 11796484
  234.0 5.8 %copy-start = (bf16[1,1,5120,384]{3,2,1,0:T(8,128)(2,1)S(1)}, bf16[1,1,5120,384]{3,2,1,0:T(8,128)(2,1)}, u32[]{:S(2)}) copy-start(bf16[1,1,5120,384]{3,2,1,0:T(8,128)(2,1)} %param.13) | copy-start | bytes 11796484
  239.8 2.3 copy-start.4
  347.1 9.8 %copy-start.2 = (bf16[16,24,5120]{2,1,0:T(8,128)(2,1)S(1)}, bf16[16,24,5120]{2,1,0:T(8,128)(2,1)}, u32[]{:S(2)}) copy-start(bf16[16,24,5120]{2,1,0:T(8,128)(2,1)} %all_to_all.25) | copy-start | bytes 11796484
  347.1 24.5 %collective-permute-start = (bf16[1,384,1280]{2,1,0:T(8,128)(2,1)S(1)}, bf16[1,384,1280]{2,1,0:T(8,128)(2,1)S(1)}, u32[]{:S(2)}, u32[]{:S(2)}) collective-permute-start(bf16[1,384,1280]{2,1,0:T(8,128)(2,1)S(1)} %fusion.13), channel_id=1, source_target_pairs={{0,64},{64,0},{1,65},{65,1},{2,66},{66,2},{3,67},{67,3},{4,68},{68... | collective-permute-start | bytes 2949128 | tf_op jit(solution)/shard_map/ppermute | solution.py:13
Sparse Core Ops, SparseCore 0:
  9.7 49.2 all-gather.2
  60.6 46.3 all-gather.4
  302.3 42.8 reduce-scatter.1
where the time goes:
time: 380 us; the launch traced here: 379 us
  waiting for transfers between devices  129 us (34%)
  blocking collectives  110 us (29%)
  local copies, waits for them, and re-layouts  60.2 us (16%)
  matrix products  37.2 us (10%)
  starting transfers between devices  16.5 us (4%)
  between operations  14.1 us (4%)
  other arithmetic  11.8 us (3%)
    all_to_all x1, blocking collectives, body(): lax.all_to_all(partial_rows, 'ep', split_axis=0, concat_axis=0, tiled=True)  57.8 us
    all_to_all x1, blocking collectives, body(): lax.all_to_all(send_x, 'ep', split_axis=0, concat_axis=0, tiled=True)  52.7 us
    all_to_all x1, waiting for transfers between devices, body(): lax.all_to_all(send_dy, 'ep', split_axis=0, concat_axis=0, tiled=True)  42.5 us
    reduce_scatter x1, waiting for transfers between devices, feature_sum(): lax.psum_scatter(terms.astype(jnp.bfloat16), 'edp', scatter_dimension=2,...  41.8 us
    all_gather x1, waiting for transfers between devices, feature_join(): lax.all_gather(pair[0], 'edp', axis=2, tiled=True)  35.4 us
    scatter x1, local copies, waits for them, and re-layouts, slot_gates(): return empty_gate.at[targets].set(block_gates.reshape(-1), mode='drop')  20.7 us
    dot_general x3, matrix products, contract_rows(): lax.dot_general(left, right, (((0,), (0,)), ((), ())), preferred_element_...  17.2 us
    gather x1, local copies, waits for them, and re-layouts, body(): jnp.take(source_dy[0], owners, axis=0, mode='fill', fill_value=0)  12.7 us
  transfers between devices with their start and end apart: 6, of which 5 were waited for; matrix products, arithmetic and copies ran while one was open for 25% of the time, Pallas kernels for 0%

commit v1 on v0

v1 whole, which is shorter than its diff:
```python
import jax
import jax.numpy as jnp
from jax import lax
from jax.experimental import pallas as pl
from jax.experimental.pallas import tpu as pltpu
from jax.sharding import PartitionSpec as P

EXPERTS = 160
TOP = 6
CAP = 24
MIB = 1 << 20


def passed_along(array, axis, by):
    length = lax.axis_size(axis)
    return lax.ppermute(array, axis, [(i, (i + by) % length) for i in range(length)])


def contract(left, right, left_dim, right_dim):
    return lax.dot_general(
        left,
        right,
        (((left_dim,), (right_dim,)), ((), ())),
        preferred_element_type=jnp.float32,
    )


def slot_choice(routes_ref, gates_ref, ep_count):
    token_count = routes_ref.shape[1]
    shape = (ep_count * CAP, token_count)
    slot = lax.broadcasted_iota(jnp.int32, (shape[0], 1), 0)
    expert = slot // CAP
    place = slot - expert * CAP
    wanted = expert * (EXPERTS // ep_count)
    named = jnp.zeros(shape, jnp.float32)
    gate = jnp.zeros(shape, jnp.float32)
    for k in range(TOP):
        hit = routes_ref[k : k + 1, :] == wanted
        named = jnp.where(hit, 1.0, named)
        if gates_ref is not None:
            gate = jnp.where(hit, gates_ref[k : k + 1, :].astype(jnp.float32), gate)
    before = lax.broadcasted_iota(jnp.int32, (token_count, token_count), 0) < (
        lax.broadcasted_iota(jnp.int32, (token_count, token_count), 1)
    )
    earlier = contract(
        named.astype(jnp.bfloat16), jnp.where(before, 1.0, 0.0).astype(jnp.bfloat16), 1, 0
    )
    chosen = (named > 0.0) & (earlier == place.astype(jnp.float32))
    one = jnp.where(chosen, 1.0, 0.0).astype(jnp.bfloat16)
    if gates_ref is None:
        return one, None
    return one, jnp.where(chosen, gate, 0.0).astype(jnp.bfloat16)


def rows_at(ref, index, count):
    return ref[pl.ds(pl.multiple_of(index * count, 128), count), :]


def columns_at(ref, index, count):
    return ref[:, pl.ds(pl.multiple_of(index * count, 128), count)]


def send_x_kernel(ep_count, routes_ref, gates_ref, x_ref, out_ref, gated_ref):
    one, gated_ref[...] = slot_choice(routes_ref, gates_ref, ep_count)
    out_ref[...] = contract(one, x_ref[...], 1, 0).astype(jnp.bfloat16)


def send_y_kernel(gated_ref, dy_ref, out_ref):
    out_ref[...] = contract(gated_ref[...], dy_ref[...], 1, 0).astype(jnp.bfloat16)


def pre_kernel(ep_count, me_ref, routes_ref, x0, x1, x2, wg_ref, wu_ref, gate_ref, up_ref, choice_ref):
    width = x0.shape[1]
    for offset, x in zip(ORDER, (x0, x1, x2)):
        at = lax.rem(me_ref[0] + offset, 4)
        gate = contract(x[...], rows_at(wg_ref, at, width), 1, 0)
        up = contract(x[...], rows_at(wu_ref, at, width), 1, 0)
        if x is x0:
            gate_ref[...] = gate
            up_ref[...] = up
        else:
            gate_ref[...] += gate
            up_ref[...] += up
    choice_ref[...], _ = slot_choice(routes_ref, None, ep_count)


def back_kernel(me_ref, y0, y2, wd_ref, back_ref):
    width = y0.shape[1]
    back_ref[...] = contract(y0[...], columns_at(wd_ref, me_ref[0], width), 1, 1)
    back_ref[...] += contract(y2[...], columns_at(wd_ref, lax.rem(me_ref[0] + 1, 4), width), 1, 1)


def mid_kernel(
    me_ref, x3, y1, y3, gate_ref, up_ref, back_ref, wg_ref, wu_ref, wd_ref,
    dg_ref, du_ref, gh_ref, p0_ref, p1_ref,
):
    width = x3.shape[1]
    left = lax.rem(me_ref[0] + 3, 4)
    far = lax.rem(me_ref[0] + 2, 4)
    wg = rows_at(wg_ref, far, width)
    wu = rows_at(wu_ref, far, width)
    gate_pre = gate_ref[...] + contract(x3[...], wg, 1, 0)
    up_pre = up_ref[...] + contract(x3[...], wu, 1, 0)
    d_hidden = (
        back_ref[...]
        + contract(y1[...], columns_at(wd_ref, left, width), 1, 1)
        + contract(y3[...], columns_at(wd_ref, far, width), 1, 1)
    )
    sigmoid = jax.nn.sigmoid(gate_pre)
    swish = gate_pre * sigmoid
    dg = (d_hidden * up_pre * sigmoid * (1.0 + gate_pre * (1.0 - sigmoid))).astype(jnp.bfloat16)
    du = (d_hidden * swish).astype(jnp.bfloat16)
    dg_ref[...] = dg
    du_ref[...] = du
    gh_ref[...] = (swish * up_pre).astype(jnp.bfloat16)
    half = width // 2
    for h, p_ref in enumerate((p0_ref, p1_ref)):
        rows = slice(h * half, (h + 1) * half)
        p_ref[...] = (contract(dg, wg[rows], 1, 1) + contract(du, wu[rows], 1, 1)).astype(
            jnp.bfloat16
        )


def part_kernel(me_ref, dg_ref, du_ref, wg_ref, wu_ref, r0_ref, r1_ref, l0_ref, l1_ref, own_ref):
    width = own_ref.shape[1]
    half = width // 2
    for offset, outs in ((1, (r0_ref, r1_ref)), (3, (l0_ref, l1_ref)), (0, (own_ref,))):
        at = lax.rem(me_ref[0] + offset, 4)
        wg = rows_at(wg_ref, at, width)
        wu = rows_at(wu_ref, at, width)
        part = contract(dg_ref[...], wg, 1, 1) + contract(du_ref[...], wu, 1, 1)
        part = part.astype(jnp.bfloat16)
        if len(outs) == 1:
            own_ref[...] = part
        else:
            outs[0][...] = part[:, :half]
            outs[1][...] = part[:, half:]


def sum_kernel(own_ref, l0_ref, l1_ref, r0_ref, r1_ref, out_ref):
    half = l0_ref.shape[1]
    rows = own_ref.shape[0]
    for h, (a, b) in enumerate(((l0_ref, r0_ref), (l1_ref, r1_ref))):
        columns = slice(h * half, (h + 1) * half)
        total = own_ref[:, columns].astype(jnp.float32)
        total = total + a[...].astype(jnp.float32) + b[...].astype(jnp.float32)
        total = total.astype(jnp.bfloat16)
        out_ref[:rows, columns] = total
        out_ref[rows:, columns] = total


def grad_kernel(me_ref, *refs):
    x, y = refs[0:4], refs[4:8]
    dg, du, gh, out_g, out_u, out_d = refs[8:]
    step = pl.program_id(0)
    for d in range(4):

        @pl.when(step == d)
        def _(d=d):
            out_g[...] = contract(x[d][...], dg[...], 0, 0).astype(jnp.bfloat16)
            out_u[...] = contract(x[d][...], du[...], 0, 0).astype(jnp.bfloat16)
            out_d[...] = contract(gh[...], y[d][...], 0, 0).astype(jnp.bfloat16)


def combine_kernel(other_ref, choice_ref, rows_ref, out_ref):
    slots = choice_ref.shape[0]
    rows = rows_at(rows_ref, other_ref[0], slots)
    out_ref[...] = contract(choice_ref[...], rows, 0, 0).astype(jnp.bfloat16)


def bf16(*shape):
    return jax.ShapeDtypeStruct(shape, jnp.bfloat16)


def f32(*shape):
    return jax.ShapeDtypeStruct(shape, jnp.float32)


IN_VMEM = pl.BlockSpec(memory_space=pltpu.VMEM)
IN_SMEM = pl.BlockSpec(memory_space=pltpu.SMEM)


def call(kernel, outs, scalars, arrays, products=0):
    return pl.pallas_call(
        kernel,
        out_shape=outs,
        in_specs=[IN_SMEM] * len(scalars) + [IN_VMEM] * len(arrays),
        out_specs=[IN_VMEM] * len(outs),
        compiler_params=pltpu.CompilerParams(vmem_limit_bytes=16 * MIB),
        cost_estimate=pl.CostEstimate(flops=4 * products, bytes_accessed=0, transcendentals=0),
    )(*scalars, *arrays)


ORDER = (0, 3, 1, 2)


def slice_at(step, me_ref):
    offset = jnp.int32(ORDER[3])
    for d in range(3):
        offset = jnp.where(step == d, ORDER[d], offset)
    return lax.rem(me_ref[0] + offset, 4)


def body(tokens, out_grads, gates, routes, w_gate, w_up, w_down):
    ep_count = lax.axis_size("ep")
    token_count, width = tokens.shape[1:]
    rows = ep_count * CAP
    hidden = w_gate.shape[3]
    half = width // 2
    one_slice = rows * width * hidden
    w_gate, w_up, w_down = w_gate[0, 0], w_up[0, 0], w_down[0, 0]
    me = lax.axis_index("edp").astype(jnp.int32).reshape(1)
    other = (1 - lax.axis_index("section")).astype(jnp.int32).reshape(1)

    routes = routes[0].T
    next_routes = passed_along(routes, "section", -1)

    send_x, gated = call(
        lambda *refs: send_x_kernel(ep_count, *refs),
        [bf16(rows, width), bf16(rows, token_count)],
        (),
        (routes, gates[0].T, tokens[0]),
        rows * token_count * (width + token_count),
    )
    (send_y,) = call(
        send_y_kernel, [bf16(rows, width)], (), (gated, out_grads[0]), rows * token_count * width
    )

    def to_experts(array):
        shaped = array.reshape(ep_count, CAP, width)
        return lax.all_to_all(shaped, "ep", split_axis=0, concat_axis=0, tiled=True).reshape(
            rows, width
        )

    own_x = to_experts(send_x)
    send_y, own_x = lax.optimization_barrier((send_y, own_x))
    x_left = passed_along(own_x, "edp", 1)
    x_right = passed_along(own_x, "edp", -1)
    own_y, x_left, x_right = lax.optimization_barrier((to_experts(send_y), x_left, x_right))
    x_far = passed_along(x_left, "edp", 1)
    y_right = passed_along(own_y, "edp", -1)
    y_left = passed_along(own_y, "edp", 1)
    y_far = passed_along(y_right, "edp", -1)

    gate_pre, up_pre, choice = call(
        lambda *refs: pre_kernel(ep_count, *refs),
        [f32(rows, hidden), f32(rows, hidden), bf16(rows, token_count)],
        (me,),
        (next_routes, own_x, x_left, x_right, w_gate, w_up),
        6 * one_slice,
    )
    (back,) = call(
        back_kernel, [f32(rows, hidden)], (me,), (own_y, y_right, w_down), 2 * one_slice
    )
    d_gate, d_up, gated_hidden, far0, far1 = call(
        mid_kernel,
        [bf16(rows, hidden)] * 3 + [bf16(rows, half)] * 2,
        (me,),
        (x_far, y_left, y_far, gate_pre, up_pre, back, w_gate, w_up, w_down),
        6 * one_slice,
    )
    far0 = passed_along(far0, "edp", 1)
    far1 = passed_along(far1, "edp", -1)
    right0, right1, left0, left1, own = call(
        part_kernel,
        [bf16(rows, half)] * 4 + [bf16(rows, width)],
        (me,),
        (d_gate, d_up, w_gate, w_up),
        6 * one_slice,
    )
    d_gate, d_up, gated_hidden, own = lax.optimization_barrier((d_gate, d_up, gated_hidden, own))

    def added(a, b):
        return (a.astype(jnp.float32) + b.astype(jnp.float32)).astype(jnp.bfloat16)

    from_left1 = passed_along(right1, "edp", 1)
    from_right0 = passed_along(left0, "edp", -1)
    from_left0 = passed_along(added(right0, far0), "edp", 1)
    from_right1 = passed_along(added(left1, far1), "edp", -1)

    x, y = (own_x, x_left, x_right, x_far), (own_y, y_left, y_right, y_far)
    smalls = (d_gate, d_up, gated_hidden)
    grad_gate, grad_up, grad_down = pl.pallas_call(
        grad_kernel,
        out_shape=[bf16(4 * width, hidden)] * 2 + [bf16(hidden, 4 * width)],
        grid_spec=pltpu.PrefetchScalarGridSpec(
            num_scalar_prefetch=1,
            grid=(4,),
            in_specs=[IN_VMEM] * 11,
            out_specs=[
                pl.BlockSpec((width, hidden), lambda i, m: (slice_at(i, m), 0)),
                pl.BlockSpec((width, hidden), lambda i, m: (slice_at(i, m), 0)),
                pl.BlockSpec((hidden, width), lambda i, m: (0, slice_at(i, m))),
            ],
        ),
        compiler_params=pltpu.CompilerParams(vmem_limit_bytes=16 * MIB),
        cost_estimate=pl.CostEstimate(
            flops=4 * 12 * one_slice, bytes_accessed=0, transcendentals=0
        ),
    )(me, *x, *y, *smalls)
    from_left0, from_right1, grad_gate, grad_up, grad_down = lax.optimization_barrier(
        (from_left0, from_right1, grad_gate, grad_up, grad_down)
    )

    (summed,) = call(
        sum_kernel,
        [bf16(2 * rows, width)],
        (),
        (own, from_left0, from_left1, from_right0, from_right1),
    )
    returned = lax.all_to_all(
        summed.reshape(2 * ep_count, CAP, width),
        ("section", "ep"),
        split_axis=0,
        concat_axis=0,
        tiled=True,
    ).reshape(2 * rows, width)
    (grad_prev,) = call(
        combine_kernel,
        [bf16(token_count, width)],
        (other,),
        (choice, returned),
        rows * token_count * width,
    )
    return (grad_prev[None], grad_gate[None, None], grad_up[None, None], grad_down[None, None])


def solution(mesh):
    placed = (
        P("section", "ep", "edp"),
        P("section", "ep", "edp"),
        P("section", "ep", None),
        P("section", "ep", None),
        P("section", "ep", None, "edp"),
        P("section", "ep", None, "edp"),
        P("section", "ep", "edp", None),
    )
    return jax.shard_map(
        body,
        mesh=mesh,
        in_specs=placed,
        out_specs=(
            P("section", "ep", "edp"),
            P("section", "ep", None, "edp"),
            P("section", "ep", None, "edp"),
            P("section", "ep", "edp", None),
        ),
        check_vma=False,
    )
```

time: 380 us -> 178 us (0.47)
  blocking collectives: 110 us -> 18.4 us
  local copies, waits for them, and re-layouts: 60.2 us -> 10.3 us
  waiting for transfers between devices: 129 us -> 80.6 us
  matrix products: 37.2 us -> 0 us
  Pallas kernels: 0 us -> 31.1 us
  starting transfers between devices: 16.5 us -> 36.5 us
  between operations: 14.1 us -> 0.77 us
  other arithmetic: 11.8 us -> 0.24 us
    all_to_all x2 -> x1, blocking collectives: 110 us -> 18.4 us  [to_experts(): lax.all_to_all(shaped, 'ep', split_axis=0, concat_axis=0, tiled=True)]
    reduce_scatter x1 -> x0, waiting for transfers between devices: 41.8 us -> none  [feature_sum(): lax.psum_scatter(terms.astype(jnp.bfloat16), 'edp', scatter_dimension=2,...]
    all_gather x2 -> x0, waiting for transfers between devices: 38.9 us -> none  [the longest x1 35.4 us: feature_join(): lax.all_gather(pair[0], 'edp', axis=2, tiled=True)]
    dot_general x9 -> x0, matrix products: 37.2 us -> none  [the longest x3 17.2 us: contract_rows(): lax.dot_general(left, right, (((0,), (0,)), ((), ())), preferred_element_...]
    ppermute x1 -> x13, waiting for transfers between devices: 4.27 us -> 39.4 us  [passed_along(): lax.ppermute(array, axis, [(i, (i + by) % length) for i in range(length)])]
    pallas_call x0 -> x9, Pallas kernels: none -> 31.1 us  [the longest x8 19.5 us: call(): pl.pallas_call(kernel, out_shape=outs, in_specs=[IN_SMEM] * len(scalars)...]
    scatter x2 -> x0, local copies, waits for them, and re-layouts: 29.8 us -> none  [the longest x1 20.7 us: slot_gates(): return empty_gate.at[targets].set(block_gates.reshape(-1), mode='drop')]
    gather x2 -> x0, local copies, waits for them, and re-layouts: 25.3 us -> none  [the longest x1 12.7 us: body(): jnp.take(source_dy[0], owners, axis=0, mode='fill', fill_value=0)]
  transfers between devices with their start and end apart: 6 -> 15, of which waited for: 5 -> 9; matrix products, arithmetic and copies ran while one was open for 25% -> 0% of each run, Pallas kernels for 0% -> 12%
where the time goes in v1:
time: 178 us
  waiting for transfers between devices  80.6 us (45%)
  starting transfers between devices  36.5 us (21%)
  Pallas kernels  31.1 us (17%)
  blocking collectives  18.4 us (10%)
  local copies, waits for them, and re-layouts  10.3 us (6%)
    ppermute x13, waiting for transfers between devices, passed_along(): lax.ppermute(array, axis, [(i, (i + by) % length) for i in range(length)])  39.4 us
    all_to_all x1, waiting for transfers between devices, body(): lax.all_to_all(summed.reshape(2 * ep_count, CAP, width), ('section', 'ep'...  26.9 us
    pallas_call x8, Pallas kernels, call(): pl.pallas_call(kernel, out_shape=outs, in_specs=[IN_SMEM] * len(scalars)...  19.5 us
    all_to_all x1, blocking collectives, to_experts(): lax.all_to_all(shaped, 'ep', split_axis=0, concat_axis=0, tiled=True)  18.4 us
    ppermute x13, starting transfers between devices, passed_along(): lax.ppermute(array, axis, [(i, (i + by) % length) for i in range(length)])  17.4 us
    all_to_all x1, waiting for transfers between devices, to_experts(): lax.all_to_all(shaped, 'ep', split_axis=0, concat_axis=0, tiled=True)  14.4 us
    pallas_call x1, Pallas kernels, body(): pl.pallas_call(grad_kernel, out_shape=[bf16(4 * width, hidden)] * 2 + [bf...  11.6 us
    all_to_all x1, starting transfers between devices, body(): lax.all_to_all(summed.reshape(2 * ep_count, CAP, width), ('section', 'ep'...  11.2 us
  transfers between devices with their start and end apart: 15, of which 9 were waited for; matrix products, arithmetic and copies ran while one was open for 0% of the time, Pallas kernels for 12%

profile of v1, /device:TPU:1, one launch (start us, length us, event | category | flops | bytes accessed | tf_op | source)
XLA Modules:
  0.0 177.9 jit_solution(8338848844279327473)
XLA Ops:
  0.6 0.7 copy.13
  1.3 1.2 copy-done.5
  2.5 0.7 copy-done.10
  3.2 2.1 %shard_map.102 = (bf16[384,1280]{1,0:T(8,128)(2,1)}, bf16[384,384]{1,0:T(8,128)(2,1)S(1)}) custom-call(s32[6,384]{1,0:T(8,128)S(1)} %bitcast.38, bf16[6,384]{1,0:T(8,128)(2,1)S(1)} %bitcast.48, bf16[384,1280]{1,0:T(8,128)(2,1)S(1)} %bitcast.46), custom_call_target="tpu_custom_call" | custom-call | flops 981467136 | tf_op jit(solution)/shard_map/pallas_call | solution.py:184
  5.4 7.8 %all-to-all-start = ((bf16[16,24,1280]{2,1,0:T(8,128)(2,1)}), bf16[16,24,1280]{2,1,0:T(8,128)(2,1)S(1)}, u32[]{:S(2)}, u32[]{:S(2)}) async-start(bf16[16,24,1280]{2,1,0:T(8,128)(2,1)} %bitcast.7), calls=%async_computation | async-start | bytes 1966080 | tf_op jit(solution)/shard_map/all_to_all | solution.py:231
  13.2 0.7 shard_map.103
  13.9 14.4 %all-to-all-done = bf16[16,24,1280]{2,1,0:T(8,128)(2,1)S(1)} async-done(((bf16[16,24,1280]{2,1,0:T(8,128)(2,1)}), bf16[16,24,1280]{2,1,0:T(8,128)(2,1)S(1)}, u32[]{:S(2)}, u32[]{:S(2)}) %all-to-all-start) | async-done | bytes 983072 | tf_op jit(solution)/shard_map/all_to_all | solution.py:231
  28.3 2.5 %collective-permute-start.2 = (bf16[384,1280]{1,0:T(8,128)(2,1)S(1)}, bf16[384,1280]{1,0:T(8,128)(2,1)S(1)}, u32[]{:S(2)}, u32[]{:S(2)}) collective-permute-start(bf16[384,1280]{1,0:T(8,128)(2,1)S(1)} %bitcast.33), channel_id=1, source_target_pairs={{0,3},{1,0},{2,1},{3,2},{4,7},{5,4},{6,5},{7,6},{8,11},{9,8},{10,9... | collective-permute-start | bytes 2949128 | tf_op jit(solution)/shard_map/ppermute | solution.py:16
  30.8 0.0 collective-permute-start.1
  30.8 18.4 %all_to_all.15 = bf16[16,24,1280]{2,1,0:T(8,128)(2,1)S(1)} all-to-all(bf16[16,24,1280]{2,1,0:T(8,128)(2,1)S(1)} %bitcast.37), channel_id=1, replica_groups=mesh['section'=2,'ep'=16,'edp'=4] {'ep'}, dimensions={0} | all-to-all | bytes 1966080 | tf_op jit(solution)/shard_map/all_to_all | solution.py:231
  49.2 1.8 %collective-permute-done.2.refs_4_.refs_2_ = bf16[384,1280]{1,0:T(8,128)(2,1)S(1)} collective-permute-done((bf16[384,1280]{1,0:T(8,128)(2,1)S(1)}, bf16[384,1280]{1,0:T(8,128)(2,1)S(1)}, u32[]{:S(2)}, u32[]{:S(2)}) %collective-permute-start.2) | collective-permute-done | bytes 983072 | tf_op jit(solution)/shard_map/ppermute | solution.py:16
  51.0 0.9 copy-done.7
  51.9 2.3 %collective-permute-done.1.refs_3_.refs_1_ = bf16[384,1280]{1,0:T(8,128)(2,1)} collective-permute-done((bf16[384,1280]{1,0:T(8,128)(2,1)S(1)}, bf16[384,1280]{1,0:T(8,128)(2,1)}, u32[]{:S(2)}, u32[]{:S(2)}) %collective-permute-start.1) | collective-permute-done | bytes 983072 | tf_op jit(solution)/shard_map/ppermute | solution.py:16
  54.2 1.1 collective-permute-start.5
  55.3 0.3 collective-permute-start.4
  55.7 0.0 collective-permute-start.3
  55.7 19.8 %collective-permute-done.5.y2.refs_6_ = bf16[384,1280]{1,0:T(8,128)(2,1)S(1)} collective-permute-done((bf16[384,1280]{1,0:T(8,128)(2,1)S(1)}, bf16[384,1280]{1,0:T(8,128)(2,1)S(1)}, u32[]{:S(2)}, u32[]{:S(2)}) %collective-permute-start.5) | collective-permute-done | bytes 983072 | tf_op jit(solution)/shard_map/ppermute | solution.py:16
  75.5 2.6 %collective-permute-start.6 = (bf16[384,1280]{1,0:T(8,128)(2,1)S(1)}, bf16[384,1280]{1,0:T(8,128)(2,1)}, u32[]{:S(2)}, u32[]{:S(2)}) collective-permute-start(bf16[384,1280]{1,0:T(8,128)(2,1)S(1)} %collective-permute-done.5.y2.refs_6_), channel_id=1, source_target_pairs={{0,3},{1,0},{2,1},{3,2},{4,7},{5,4},{6,5},{7,6},{8,11},{9,8},{10,9... | collective-permute-start | bytes 2949128 | tf_op jit(solution)/shard_map/ppermute | solution.py:16
  78.0 2.6 %collective-permute-start = (s32[6,384]{1,0:T(8,128)S(1)}, s32[6,384]{1,0:T(8,128)S(1)}, u32[]{:S(2)}, u32[]{:S(2)}) collective-permute-start(s32[6,384]{1,0:T(8,128)S(1)} %bitcast.39), channel_id=1, source_target_pairs={{0,64},{64,0},{1,65},{65,1},{2,66},{66,2},{3,67},{67,3},{4,68},{68... | collective-permute-start | bytes 27656 | tf_op jit(solution)/shard_map/ppermute | solution.py:16
  80.7 1.4 collective-permute-done.refs_1_
  82.1 2.1 %copy-done.2 = bf16[1,1,5120,384]{3,2,1,0:T(8,128)(2,1)S(1)} copy-done((bf16[1,1,5120,384]{3,2,1,0:T(8,128)(2,1)S(1)}, bf16[1,1,5120,384]{3,2,1,0:T(8,128)(2,1)}, u32[]{:S(2)}) %copy-start.2) | copy-done | bytes 3932184
  84.2 2.1 %copy-done.3 = bf16[1,1,5120,384]{3,2,1,0:T(8,128)(2,1)S(1)} copy-done((bf16[1,1,5120,384]{3,2,1,0:T(8,128)(2,1)S(1)}, bf16[1,1,5120,384]{3,2,1,0:T(8,128)(2,1)}, u32[]{:S(2)}) %copy-start.3) | copy-done | bytes 3932184
  86.3 1.2 copy-done.8
  87.5 4.8 %shard_map.104 = (f32[384,384]{1,0:T(8,128)S(1)}, f32[384,384]{1,0:T(8,128)S(1)}, bf16[384,384]{1,0:T(8,128)(2,1)S(1)}) custom-call(s32[1]{0:T(128)} %bitcast.1.refs_0_.me_ref, s32[6,384]{1,0:T(8,128)S(1)} %collective-permute-done.refs_1_, bf16[384,1280]{1,0:T(8,128)(2,1)S(1)} %bitcast.35, bf16[384,1280]{1,0:T(8,128)(2,1)} %collective-permute-done.1.refs_3_.refs_1_, ...), custom_call_target="tpu_custom_call" | custom-call | flops 4529848320 | tf_op jit(solution)/shard_map/pallas_call | solution.py:184
  92.3 0.0 copy-start.4
  92.4 1.2 shard_map.105.back_ref
  93.6 5.4 %collective-permute-done.3.x3.refs_3_ = bf16[384,1280]{1,0:T(8,128)(2,1)} collective-permute-done((bf16[384,1280]{1,0:T(8,128)(2,1)}, bf16[384,1280]{1,0:T(8,128)(2,1)}, u32[]{:S(2)}, u32[]{:S(2)}) %collective-permute-start.3) | collective-permute-done | bytes 983072 | tf_op jit(solution)/shard_map/ppermute | solution.py:16
  98.9 0.0 collective-permute-done.6.y3.refs_7_
  98.9 5.4 %shard_map.106 = (bf16[384,384]{1,0:T(8,128)(2,1)S(1)}, bf16[384,384]{1,0:T(8,128)(2,1)S(1)}, bf16[384,384]{1,0:T(8,128)(2,1)S(1)}, bf16[384,640]{1,0:T(8,128)(2,1)S(1)}, bf16[384,640]{1,0:T(8,128)(2,1)S(1)}) custom-call(s32[1]{0:T(128)} %bitcast.1.refs_0_.me_ref, bf16[384,1280]{1,0:T(8,128)(2,1)} %collective-permute-done.3.x3.refs_3_, ...), custom_call_target="tpu_custom_call" | custom-call | flops 4529848320 | tf_op jit(solution)/shard_map/pallas_call | solution.py:184
  104.3 0.1 collective-permute-start.7
  104.4 2.7 %collective-permute-start.9 = (bf16[384,640]{1,0:T(8,128)(2,1)S(1)}, bf16[384,640]{1,0:T(8,128)(2,1)S(1)}, u32[]{:S(2)}, u32[]{:S(2)}) collective-permute-start(bf16[384,640]{1,0:T(8,128)(2,1)S(1)} %get-tuple-element.54), channel_id=1, source_target_pairs={{0,3},{1,0},{2,1},{3,2},{4,7},{5,4},{6,5},{7,6},{8,11},{9,8},{10,9... | collective-permute-start | bytes 1474568 | tf_op jit(solution)/shard_map/ppermute | solution.py:16
  107.1 3.2 %shard_map.107 = (bf16[384,640]{1,0:T(8,128)(2,1)S(1)}, bf16[384,640]{1,0:T(8,128)(2,1)S(1)}, bf16[384,640]{1,0:T(8,128)(2,1)S(1)}, bf16[384,640]{1,0:T(8,128)(2,1)S(1)}, bf16[384,1280]{1,0:T(8,128)(2,1)S(1)}) custom-call(s32[1]{0:T(128)} %bitcast.1.refs_0_.me_ref, bf16[384,384]{1,0:T(8,128)(2,1)S(1)} %get-tuple-element.55.dg_ref.refs_8_, ...), custom_call_target="tpu_custom_call" | custom-call | flops 4529848320 | tf_op jit(solution)/shard_map/pallas_call | solution.py:184
  110.3 0.1 collective-permute-start.11
  110.4 2.7 %collective-permute-start.12 = (bf16[384,640]{1,0:T(8,128)(2,1)S(1)}, bf16[384,640]{1,0:T(8,128)(2,1)S(1)}, u32[]{:S(2)}, u32[]{:S(2)}) collective-permute-start(bf16[384,640]{1,0:T(8,128)(2,1)S(1)} %get-tuple-element.63), channel_id=1, source_target_pairs={{0,3},{1,0},{2,1},{3,2},{4,7},{5,4},{6,5},{7,6},{8,11},{9,8},{10,9... | collective-permute-start | bytes 1474568 | tf_op jit(solution)/shard_map/ppermute | solution.py:16
  113.1 2.3 %collective-permute-done.7 = bf16[384,640]{1,0:T(8,128)(2,1)S(1)} collective-permute-done((bf16[384,640]{1,0:T(8,128)(2,1)S(1)}, bf16[384,640]{1,0:T(8,128)(2,1)S(1)}, u32[]{:S(2)}, u32[]{:S(2)}) %collective-permute-start.7) | collective-permute-done | bytes 491552 | tf_op jit(solution)/shard_map/ppermute | solution.py:16
  115.3 0.1 add_convert_fusion.1
  115.4 0.1 collective-permute-start.8
  115.5 0.0 collective-permute-done.9
  115.5 0.1 add_convert_fusion
  115.7 2.7 %collective-permute-start.10 = (bf16[384,640]{1,0:T(8,128)(2,1)S(1)}, bf16[384,640]{1,0:T(8,128)(2,1)S(1)}, u32[]{:S(2)}, u32[]{:S(2)}) collective-permute-start(bf16[384,640]{1,0:T(8,128)(2,1)S(1)} %add_convert_fusion), channel_id=1, source_target_pairs={{0,3},{1,0},{2,1},{3,2},{4,7},{5,4},{6,5},{7,6},{8,11},{9,8},{10,9... | collective-permute-start | bytes 1474568 | tf_op jit(solution)/shard_map/ppermute | solution.py:16
  118.4 11.6 %shard_map.108 = (bf16[5120,384]{1,0:T(8,128)(2,1)}, bf16[5120,384]{1,0:T(8,128)(2,1)}, bf16[384,5120]{1,0:T(8,128)(2,1)}) custom-call(s32[1]{0:T(128)} %bitcast.1.refs_0_.me_ref, bf16[384,1280]{1,0:T(8,128)(2,1)S(1)} %bitcast.36, bf16[384,1280]{1,0:T(8,128)(2,1)} %collective-permute-done.1.refs_3_.refs_1_, bf16[384,1280]{1,0:T(8,128)(2,1)S(1)} %copy-done.9, ...), custom_call_target="tpu_custom_call" | custom-call | flops 9059696640 | tf_op jit(solution)/shard_map/pallas_call | solution.py:283
  130.0 6.4 %collective-permute-done.8.l0_ref = bf16[384,640]{1,0:T(8,128)(2,1)S(1)} collective-permute-done((bf16[384,640]{1,0:T(8,128)(2,1)S(1)}, bf16[384,640]{1,0:T(8,128)(2,1)S(1)}, u32[]{:S(2)}, u32[]{:S(2)}) %collective-permute-start.8) | collective-permute-done | bytes 491552 | tf_op jit(solution)/shard_map/ppermute | solution.py:16
  136.4 0.0 collective-permute-done.12.r0_ref
  136.4 0.4 shard_map.109
  136.8 1.3 copy-done
  138.1 11.2 %all-to-all-start.2 = ((bf16[32,24,1280]{2,1,0:T(8,128)(2,1)}), bf16[32,24,1280]{2,1,0:T(8,128)(2,1)S(1)}, u32[]{:S(2)}, u32[]{:S(2)}) async-start(bf16[32,24,1280]{2,1,0:T(8,128)(2,1)} %bitcast.26), calls=%async_computation.2 | async-start | bytes 3932160 | tf_op jit(solution)/shard_map/all_to_all | solution.py:311
  149.3 26.9 %all-to-all-done.2 = bf16[32,24,1280]{2,1,0:T(8,128)(2,1)S(1)} async-done(((bf16[32,24,1280]{2,1,0:T(8,128)(2,1)}), bf16[32,24,1280]{2,1,0:T(8,128)(2,1)S(1)}, u32[]{:S(2)}, u32[]{:S(2)}) %all-to-all-start.2) | async-done | bytes 1966112 | tf_op jit(solution)/shard_map/all_to_all | solution.py:311
  176.2 1.7 shard_map.110
  (17 shorter events, 0.0 us)
Async XLA Ops:
  1.3 1.2 copy-start.5
  2.5 0.7 copy-start.10
  3.2 10.0 %copy-start.6 = (bf16[1,384,1280]{2,1,0:T(8,128)(2,1)S(1)}, bf16[1,384,1280]{2,1,0:T(8,128)(2,1)}, u32[]{:S(2)}) copy-start(bf16[1,384,1280]{2,1,0:T(8,128)(2,1)} %param.8) | copy-start | bytes 2949124
  5.4 22.9 %all-to-all-start = ((bf16[16,24,1280]{2,1,0:T(8,128)(2,1)}), bf16[16,24,1280]{2,1,0:T(8,128)(2,1)S(1)}, u32[]{:S(2)}, u32[]{:S(2)}) async-start(bf16[16,24,1280]{2,1,0:T(8,128)(2,1)} %bitcast.7), calls=%async_computation | async-start | bytes 1966080 | tf_op jit(solution)/shard_map/all_to_all | solution.py:231
  28.3 22.7 %collective-permute-start.2 = (bf16[384,1280]{1,0:T(8,128)(2,1)S(1)}, bf16[384,1280]{1,0:T(8,128)(2,1)S(1)}, u32[]{:S(2)}, u32[]{:S(2)}) collective-permute-start(bf16[384,1280]{1,0:T(8,128)(2,1)S(1)} %bitcast.33), channel_id=1, source_target_pairs={{0,3},{1,0},{2,1},{3,2},{4,7},{5,4},{6,5},{7,6},{8,11},{9,8},{10,9... | collective-permute-start | bytes 2949128 | tf_op jit(solution)/shard_map/ppermute | solution.py:16
  30.8 23.4 %collective-permute-start.1 = (bf16[384,1280]{1,0:T(8,128)(2,1)S(1)}, bf16[384,1280]{1,0:T(8,128)(2,1)}, u32[]{:S(2)}, u32[]{:S(2)}) collective-permute-start(bf16[384,1280]{1,0:T(8,128)(2,1)S(1)} %bitcast.34), channel_id=1, source_target_pairs={{0,1},{1,2},{2,3},{3,0},{4,5},{5,6},{6,7},{7,4},{8,9},{9,10},{10,1... | collective-permute-start | bytes 2949128 | tf_op jit(solution)/shard_map/ppermute | solution.py:16
  51.0 0.9 copy-start.7
  54.2 21.3 %collective-permute-start.5 = (bf16[384,1280]{1,0:T(8,128)(2,1)S(1)}, bf16[384,1280]{1,0:T(8,128)(2,1)S(1)}, u32[]{:S(2)}, u32[]{:S(2)}) collective-permute-start(bf16[384,1280]{1,0:T(8,128)(2,1)S(1)} %bitcast.27), channel_id=1, source_target_pairs={{0,3},{1,0},{2,1},{3,2},{4,7},{5,4},{6,5},{7,6},{8,11},{9,8},{10,9... | collective-permute-start | bytes 2949128 | tf_op jit(solution)/shard_map/ppermute | solution.py:16
  55.3 43.6 %collective-permute-start.4 = (bf16[384,1280]{1,0:T(8,128)(2,1)S(1)}, bf16[384,1280]{1,0:T(8,128)(2,1)}, u32[]{:S(2)}, u32[]{:S(2)}) collective-permute-start(bf16[384,1280]{1,0:T(8,128)(2,1)S(1)} %bitcast.28), channel_id=1, source_target_pairs={{0,1},{1,2},{2,3},{3,0},{4,5},{5,6},{6,7},{7,4},{8,9},{9,10},{10,1... | collective-permute-start | bytes 2949128 | tf_op jit(solution)/shard_map/ppermute | solution.py:16
  55.7 43.3 %collective-permute-start.3 = (bf16[384,1280]{1,0:T(8,128)(2,1)}, bf16[384,1280]{1,0:T(8,128)(2,1)}, u32[]{:S(2)}, u32[]{:S(2)}) collective-permute-start(bf16[384,1280]{1,0:T(8,128)(2,1)} %collective-permute-done.1.refs_3_.refs_1_), channel_id=1, source_target_pairs={{0,1},{1,2},{2,3},{3,0},{4,5},{5,6},{6,7},{7,4},{8,9},{9,10},{10,1... | collective-permute-start | bytes 2949128 | tf_op jit(solution)/shard_map/ppermute | solution.py:16
  75.5 23.4 %collective-permute-start.6 = (bf16[384,1280]{1,0:T(8,128)(2,1)S(1)}, bf16[384,1280]{1,0:T(8,128)(2,1)}, u32[]{:S(2)}, u32[]{:S(2)}) collective-permute-start(bf16[384,1280]{1,0:T(8,128)(2,1)S(1)} %collective-permute-done.5.y2.refs_6_), channel_id=1, source_target_pairs={{0,3},{1,0},{2,1},{3,2},{4,7},{5,4},{6,5},{7,6},{8,11},{9,8},{10,9... | collective-permute-start | bytes 2949128 | tf_op jit(solution)/shard_map/ppermute | solution.py:16
  78.0 4.0 %collective-permute-start = (s32[6,384]{1,0:T(8,128)S(1)}, s32[6,384]{1,0:T(8,128)S(1)}, u32[]{:S(2)}, u32[]{:S(2)}) collective-permute-start(s32[6,384]{1,0:T(8,128)S(1)} %bitcast.39), channel_id=1, source_target_pairs={{0,64},{64,0},{1,65},{65,1},{2,66},{66,2},{3,67},{67,3},{4,68},{68... | collective-permute-start | bytes 27656 | tf_op jit(solution)/shard_map/ppermute | solution.py:16
  82.1 2.1 %copy-start.2 = (bf16[1,1,5120,384]{3,2,1,0:T(8,128)(2,1)S(1)}, bf16[1,1,5120,384]{3,2,1,0:T(8,128)(2,1)}, u32[]{:S(2)}) copy-start(bf16[1,1,5120,384]{3,2,1,0:T(8,128)(2,1)} %param.11) | copy-start | bytes 11796484
  84.2 2.1 %copy-start.3 = (bf16[1,1,5120,384]{3,2,1,0:T(8,128)(2,1)S(1)}, bf16[1,1,5120,384]{3,2,1,0:T(8,128)(2,1)}, u32[]{:S(2)}) copy-start(bf16[1,1,5120,384]{3,2,1,0:T(8,128)(2,1)} %param.12) | copy-start | bytes 11796484
  86.3 1.2 copy-start.8
  87.5 4.8 %copy-start.1 = (bf16[1,1,384,5120]{3,2,1,0:T(8,128)(2,1)S(1)}, bf16[1,1,384,5120]{3,2,1,0:T(8,128)(2,1)}, u32[]{:S(2)}) copy-start(bf16[1,1,384,5120]{3,2,1,0:T(8,128)(2,1)} %param.13) | copy-start | bytes 11796484
  92.3 6.6 %copy-start.4 = (bf16[1,1,5120,384]{3,2,1,0:T(8,128)(2,1)S(1)}, bf16[1,1,5120,384]{3,2,1,0:T(8,128)(2,1)}, u32[]{:S(2)}) copy-start(bf16[1,1,5120,384]{3,2,1,0:T(8,128)(2,1)} %param.12) | copy-start | bytes 11796484
  104.3 11.0 %collective-permute-start.7 = (bf16[384,640]{1,0:T(8,128)(2,1)S(1)}, bf16[384,640]{1,0:T(8,128)(2,1)S(1)}, u32[]{:S(2)}, u32[]{:S(2)}) collective-permute-start(bf16[384,640]{1,0:T(8,128)(2,1)S(1)} %get-tuple-element.52), channel_id=1, source_target_pairs={{0,1},{1,2},{2,3},{3,0},{4,5},{5,6},{6,7},{7,4},{8,9},{9,10},{10,1... | collective-permute-start | bytes 1474568 | tf_op jit(solution)/shard_map/ppermute | solution.py:16
  104.4 11.1 %collective-permute-start.9 = (bf16[384,640]{1,0:T(8,128)(2,1)S(1)}, bf16[384,640]{1,0:T(8,128)(2,1)S(1)}, u32[]{:S(2)}, u32[]{:S(2)}) collective-permute-start(bf16[384,640]{1,0:T(8,128)(2,1)S(1)} %get-tuple-element.54), channel_id=1, source_target_pairs={{0,3},{1,0},{2,1},{3,2},{4,7},{5,4},{6,5},{7,6},{8,11},{9,8},{10,9... | collective-permute-start | bytes 1474568 | tf_op jit(solution)/shard_map/ppermute | solution.py:16
  107.1 11.3 %copy-start.9 = (bf16[384,1280]{1,0:T(8,128)(2,1)S(1)}, bf16[384,1280]{1,0:T(8,128)(2,1)}, u32[]{:S(2)}) copy-start(bf16[384,1280]{1,0:T(8,128)(2,1)} %copy-done.7) | copy-start | bytes 2949124
  110.3 26.1 %collective-permute-start.11 = (bf16[384,640]{1,0:T(8,128)(2,1)S(1)}, bf16[384,640]{1,0:T(8,128)(2,1)S(1)}, u32[]{:S(2)}, u32[]{:S(2)}) collective-permute-start(bf16[384,640]{1,0:T(8,128)(2,1)S(1)} %get-tuple-element.62), channel_id=1, source_target_pairs={{0,1},{1,2},{2,3},{3,0},{4,5},{5,6},{6,7},{7,4},{8,9},{9,10},{10,1... | collective-permute-start | bytes 1474568 | tf_op jit(solution)/shard_map/ppermute | solution.py:16
  110.4 26.0 %collective-permute-start.12 = (bf16[384,640]{1,0:T(8,128)(2,1)S(1)}, bf16[384,640]{1,0:T(8,128)(2,1)S(1)}, u32[]{:S(2)}, u32[]{:S(2)}) collective-permute-start(bf16[384,640]{1,0:T(8,128)(2,1)S(1)} %get-tuple-element.63), channel_id=1, source_target_pairs={{0,3},{1,0},{2,1},{3,2},{4,7},{5,4},{6,5},{7,6},{8,11},{9,8},{10,9... | collective-permute-start | bytes 1474568 | tf_op jit(solution)/shard_map/ppermute | solution.py:16
  115.4 20.9 %collective-permute-start.8 = (bf16[384,640]{1,0:T(8,128)(2,1)S(1)}, bf16[384,640]{1,0:T(8,128)(2,1)S(1)}, u32[]{:S(2)}, u32[]{:S(2)}) collective-permute-start(bf16[384,640]{1,0:T(8,128)(2,1)S(1)} %add_convert_fusion.1), channel_id=1, source_target_pairs={{0,1},{1,2},{2,3},{3,0},{4,5},{5,6},{6,7},{7,4},{8,9},{9,10},{10,1... | collective-permute-start | bytes 1474568 | tf_op jit(solution)/shard_map/ppermute | solution.py:16
  115.7 20.7 %collective-permute-start.10 = (bf16[384,640]{1,0:T(8,128)(2,1)S(1)}, bf16[384,640]{1,0:T(8,128)(2,1)S(1)}, u32[]{:S(2)}, u32[]{:S(2)}) collective-permute-start(bf16[384,640]{1,0:T(8,128)(2,1)S(1)} %add_convert_fusion), channel_id=1, source_target_pairs={{0,3},{1,0},{2,1},{3,2},{4,7},{5,4},{6,5},{7,6},{8,11},{9,8},{10,9... | collective-permute-start | bytes 1474568 | tf_op jit(solution)/shard_map/ppermute | solution.py:16
  136.8 1.3 copy-start
  138.1 38.1 %all-to-all-start.2 = ((bf16[32,24,1280]{2,1,0:T(8,128)(2,1)}), bf16[32,24,1280]{2,1,0:T(8,128)(2,1)S(1)}, u32[]{:S(2)}, u32[]{:S(2)}) async-start(bf16[32,24,1280]{2,1,0:T(8,128)(2,1)} %bitcast.26), calls=%async_computation.2 | async-start | bytes 3932160 | tf_op jit(solution)/shard_map/all_to_all | solution.py:311

commit v2 on v1

--- a/solution.py
+++ b/solution.py
@@ -84,28 +84,35 @@
     choice_ref[...], _ = slot_choice(routes_ref, None, ep_count)
 
 
-def back_kernel(me_ref, y0, y2, wd_ref, back_ref):
+def back_kernel(me_ref, y0, y1, y2, wd_ref, back_ref):
     width = y0.shape[1]
-    back_ref[...] = contract(y0[...], columns_at(wd_ref, me_ref[0], width), 1, 1)
-    back_ref[...] += contract(y2[...], columns_at(wd_ref, lax.rem(me_ref[0] + 1, 4), width), 1, 1)
+    for offset, y in zip(ORDER, (y0, y1, y2)):
+        at = lax.rem(me_ref[0] + offset, 4)
+        back = contract(y[...], columns_at(wd_ref, at, width), 1, 1)
+        if y is y0:
+            back_ref[...] = back
+        else:
+            back_ref[...] += back
 
 
 def mid_kernel(
-    me_ref, x3, y1, y3, gate_ref, up_ref, back_ref, wg_ref, wu_ref, wd_ref,
+    me_ref, x30, x31, y30, y31, gate_ref, up_ref, back_ref, wg_ref, wu_ref, wd_ref,
     dg_ref, du_ref, gh_ref, p0_ref, p1_ref,
 ):
-    width = x3.shape[1]
-    left = lax.rem(me_ref[0] + 3, 4)
+    half = x30.shape[1]
+    width = 2 * half
     far = lax.rem(me_ref[0] + 2, 4)
     wg = rows_at(wg_ref, far, width)
     wu = rows_at(wu_ref, far, width)
-    gate_pre = gate_ref[...] + contract(x3[...], wg, 1, 0)
-    up_pre = up_ref[...] + contract(x3[...], wu, 1, 0)
-    d_hidden = (
-        back_ref[...]
-        + contract(y1[...], columns_at(wd_ref, left, width), 1, 1)
-        + contract(y3[...], columns_at(wd_ref, far, width), 1, 1)
-    )
+    wd = columns_at(wd_ref, far, width)
+    gate_pre = gate_ref[...]
+    up_pre = up_ref[...]
+    d_hidden = back_ref[...]
+    for h, (x, y) in enumerate(((x30, y30), (x31, y31))):
+        span = slice(h * half, (h + 1) * half)
+        gate_pre += contract(x[...], wg[span], 1, 0)
+        up_pre += contract(x[...], wu[span], 1, 0)
+        d_hidden += contract(y[...], wd[:, span], 1, 1)
     sigmoid = jax.nn.sigmoid(gate_pre)
     swish = gate_pre * sigmoid
     dg = (d_hidden * up_pre * sigmoid * (1.0 + gate_pre * (1.0 - sigmoid))).astype(jnp.bfloat16)
@@ -113,7 +120,6 @@
     dg_ref[...] = dg
     du_ref[...] = du
     gh_ref[...] = (swish * up_pre).astype(jnp.bfloat16)
-    half = width // 2
     for h, p_ref in enumerate((p0_ref, p1_ref)):
         rows = slice(h * half, (h + 1) * half)
         p_ref[...] = (contract(dg, wg[rows], 1, 1) + contract(du, wu[rows], 1, 1)).astype(
@@ -150,16 +156,19 @@
 
 
 def grad_kernel(me_ref, *refs):
-    x, y = refs[0:4], refs[4:8]
-    dg, du, gh, out_g, out_u, out_d = refs[8:]
+    x, y = refs[0:5], refs[5:10]
+    dg, du, gh, out_g, out_u, out_d = refs[10:]
     step = pl.program_id(0)
     for d in range(4):
 
         @pl.when(step == d)
         def _(d=d):
-            out_g[...] = contract(x[d][...], dg[...], 0, 0).astype(jnp.bfloat16)
-            out_u[...] = contract(x[d][...], du[...], 0, 0).astype(jnp.bfloat16)
-            out_d[...] = contract(gh[...], y[d][...], 0, 0).astype(jnp.bfloat16)
+            for n, (x_ref, y_ref) in enumerate(zip(x[d : d + 1 + d // 3], y[d : d + 1 + d // 3])):
+                count = x_ref.shape[1]
+                span = slice(n * count, (n + 1) * count)
+                out_g[span, :] = contract(x_ref[...], dg[...], 0, 0).astype(jnp.bfloat16)
+                out_u[span, :] = contract(x_ref[...], du[...], 0, 0).astype(jnp.bfloat16)
+                out_d[:, span] = contract(gh[...], y_ref[...], 0, 0).astype(jnp.bfloat16)
 
 
 def combine_kernel(other_ref, choice_ref, rows_ref, out_ref):
@@ -178,6 +187,14 @@
 
 IN_VMEM = pl.BlockSpec(memory_space=pltpu.VMEM)
 IN_SMEM = pl.BlockSpec(memory_space=pltpu.SMEM)
+
+
+def whole(array):
+    return pl.BlockSpec(array.shape, lambda *_: (0,) * len(array.shape), pipeline_mode=pl.Buffered(1))
+
+
+def in_hbm(array):
+    return pltpu.with_memory_space_constraint(array, pltpu.HBM)
 
 
 def call(kernel, outs, scalars, arrays, products=0):
@@ -212,7 +229,7 @@
     me = lax.axis_index("edp").astype(jnp.int32).reshape(1)
     other = (1 - lax.axis_index("section")).astype(jnp.int32).reshape(1)
 
-    routes = routes[0].T
+    routes, me, other = lax.optimization_barrier((routes[0].T, me, other))
     next_routes = passed_along(routes, "section", -1)
 
     send_x, gated = call(
@@ -237,10 +254,10 @@
     x_left = passed_along(own_x, "edp", 1)
     x_right = passed_along(own_x, "edp", -1)
     own_y, x_left, x_right = lax.optimization_barrier((to_experts(send_y), x_left, x_right))
-    x_far = passed_along(x_left, "edp", 1)
+    x_far0 = passed_along(x_left[:, :half], "edp", 1)
+    x_far1 = passed_along(x_right[:, half:], "edp", -1)
     y_right = passed_along(own_y, "edp", -1)
     y_left = passed_along(own_y, "edp", 1)
-    y_far = passed_along(y_right, "edp", -1)
 
     gate_pre, up_pre, choice = call(
         lambda *refs: pre_kernel(ep_count, *refs),
@@ -249,15 +266,24 @@
         (next_routes, own_x, x_left, x_right, w_gate, w_up),
         6 * one_slice,
     )
+    y_left, y_right, gate_pre, up_pre, choice = lax.optimization_barrier(
+        (y_left, y_right, gate_pre, up_pre, choice)
+    )
+    y_far0 = passed_along(y_left[:, :half], "edp", 1)
+    y_far1 = passed_along(y_right[:, half:], "edp", -1)
     (back,) = call(
-        back_kernel, [f32(rows, hidden)], (me,), (own_y, y_right, w_down), 2 * one_slice
+        back_kernel,
+        [f32(rows, hidden)],
+        (me,),
+        (own_y, y_left, y_right, w_down),
+        3 * one_slice,
     )
     d_gate, d_up, gated_hidden, far0, far1 = call(
         mid_kernel,
         [bf16(rows, hidden)] * 3 + [bf16(rows, half)] * 2,
         (me,),
-        (x_far, y_left, y_far, gate_pre, up_pre, back, w_gate, w_up, w_down),
-        6 * one_slice,
+        (x_far0, x_far1, y_far0, y_far1, gate_pre, up_pre, back, w_gate, w_up, w_down),
+        5 * one_slice,
     )
     far0 = passed_along(far0, "edp", 1)
     far1 = passed_along(far1, "edp", -1)
@@ -268,7 +294,6 @@
         (d_gate, d_up, w_gate, w_up),
         6 * one_slice,
     )
-    d_gate, d_up, gated_hidden, own = lax.optimization_barrier((d_gate, d_up, gated_hidden, own))
 
     def added(a, b):
         return (a.astype(jnp.float32) + b.astype(jnp.float32)).astype(jnp.bfloat16)
@@ -278,7 +303,17 @@
     from_left0 = passed_along(added(right0, far0), "edp", 1)
     from_right1 = passed_along(added(left1, far1), "edp", -1)
 
-    x, y = (own_x, x_left, x_right, x_far), (own_y, y_left, y_right, y_far)
+    (summed,) = call(
+        sum_kernel,
+        [bf16(2 * rows, width)],
+        (),
+        (own, from_left0, from_left1, from_right0, from_right1),
+    )
+    summed, d_gate, d_up, gated_hidden = lax.optimization_barrier(
+        (summed, d_gate, d_up, gated_hidden)
+    )
+    x = (own_x, x_left, x_right, x_far0, x_far1)
+    y = (own_y, y_left, y_right, y_far0, y_far1)
     smalls = (d_gate, d_up, gated_hidden)
     grad_gate, grad_up, grad_down = pl.pallas_call(
         grad_kernel,
@@ -286,28 +321,18 @@
         grid_spec=pltpu.PrefetchScalarGridSpec(
             num_scalar_prefetch=1,
             grid=(4,),
-            in_specs=[IN_VMEM] * 11,
+            in_specs=[whole(a) for a in (*x, *y, *smalls)],
             out_specs=[
                 pl.BlockSpec((width, hidden), lambda i, m: (slice_at(i, m), 0)),
                 pl.BlockSpec((width, hidden), lambda i, m: (slice_at(i, m), 0)),
                 pl.BlockSpec((hidden, width), lambda i, m: (0, slice_at(i, m))),
             ],
         ),
-        compiler_params=pltpu.CompilerParams(vmem_limit_bytes=16 * MIB),
+        compiler_params=pltpu.CompilerParams(vmem_limit_bytes=28 * MIB),
         cost_estimate=pl.CostEstimate(
             flops=4 * 12 * one_slice, bytes_accessed=0, transcendentals=0
         ),
-    )(me, *x, *y, *smalls)
-    from_left0, from_right1, grad_gate, grad_up, grad_down = lax.optimization_barrier(
-        (from_left0, from_right1, grad_gate, grad_up, grad_down)
-    )
-
-    (summed,) = call(
-        sum_kernel,
-        [bf16(2 * rows, width)],
-        (),
-        (own, from_left0, from_left1, from_right0, from_right1),
-    )
+    )(me, *(in_hbm(a) for a in (*x, *y, *smalls)))
     returned = lax.all_to_all(
         summed.reshape(2 * ep_count, CAP, width),
         ("section", "ep"),

time: 178 us -> 176 us (0.989)
  local copies, waits for them, and re-layouts: 10.3 us -> 6.99 us
    ppermute x13 -> x15, waiting for transfers between devices: 39.4 us -> 54.2 us  [passed_along(): lax.ppermute(array, axis, [(i, (i + by) % length) for i in range(length)])]
    all_to_all x1, waiting for transfers between devices: 26.9 us -> 13.7 us  [body(): lax.all_to_all(summed.reshape(2 * ep_count, CAP, width), ('section', 'ep'...]
    unnamed x23 -> x47, local copies, waits for them, and re-layouts: 10.3 us -> 6.82 us
    pallas_call x8, Pallas kernels: 19.5 us -> 16.6 us  [call(): pl.pallas_call(kernel, out_shape=outs, in_specs=[IN_SMEM] * len(scalars)...]
    ppermute x13 -> x15, starting transfers between devices: 17.4 us -> 18 us  [passed_along(): lax.ppermute(array, axis, [(i, (i + by) % length) for i in range(length)])]
  transfers between devices with their start and end apart: 15 -> 17, of which waited for: 9 -> 13; matrix products, arithmetic and copies ran while one was open for 0% -> 0% of each run, Pallas kernels for 12% -> 13%
where the time goes in v2:
time: 176 us
  waiting for transfers between devices  82.3 us (47%)
  starting transfers between devices  37 us (21%)
  Pallas kernels  29.7 us (17%)
  blocking collectives  18.4 us (10%)
  local copies, waits for them, and re-layouts  6.99 us (4%)
    ppermute x15, waiting for transfers between devices, passed_along(): lax.ppermute(array, axis, [(i, (i + by) % length) for i in range(length)])  54.2 us
    all_to_all x1, blocking collectives, to_experts(): lax.all_to_all(shaped, 'ep', split_axis=0, concat_axis=0, tiled=True)  18.4 us
    ppermute x15, starting transfers between devices, passed_along(): lax.ppermute(array, axis, [(i, (i + by) % length) for i in range(length)])  18 us
    pallas_call x8, Pallas kernels, call(): pl.pallas_call(kernel, out_shape=outs, in_specs=[IN_SMEM] * len(scalars)...  16.6 us
    all_to_all x1, waiting for transfers between devices, to_experts(): lax.all_to_all(shaped, 'ep', split_axis=0, concat_axis=0, tiled=True)  14.4 us
    all_to_all x1, waiting for transfers between devices, body(): lax.all_to_all(summed.reshape(2 * ep_count, CAP, width), ('section', 'ep'...  13.7 us
    pallas_call x1, Pallas kernels, body(): pl.pallas_call(grad_kernel, out_shape=[bf16(4 * width, hidden)] * 2 + [bf...  13.2 us
    all_to_all x1, starting transfers between devices, body(): lax.all_to_all(summed.reshape(2 * ep_count, CAP, width), ('section', 'ep'...  11.2 us
  transfers between devices with their start and end apart: 17, of which 13 were waited for; matrix products, arithmetic and copies ran while one was open for 0% of the time, Pallas kernels for 13%

profile of v2, /device:TPU:1, one launch (start us, length us, event | category | flops | bytes accessed | tf_op | source)
XLA Modules:
  0.0 175.6 jit_solution(11415698260636663058)
XLA Ops:
  0.6 0.7 copy.13
  1.3 1.2 copy-done.17
  2.5 0.7 copy-done.22
  3.2 2.1 %shard_map.102 = (bf16[384,1280]{1,0:T(8,128)(2,1)}, bf16[384,384]{1,0:T(8,128)(2,1)S(1)}) custom-call(s32[6,384]{1,0:T(8,128)S(1)} %bitcast.44, bf16[6,384]{1,0:T(8,128)(2,1)S(1)} %bitcast.48, bf16[384,1280]{1,0:T(8,128)(2,1)S(1)} %bitcast.46), custom_call_target="tpu_custom_call" | custom-call | flops 981467136 | tf_op jit(solution)/shard_map/pallas_call | solution.py:201
  5.4 7.8 %all-to-all-start = ((bf16[16,24,1280]{2,1,0:T(8,128)(2,1)}), bf16[16,24,1280]{2,1,0:T(8,128)(2,1)S(1)}, u32[]{:S(2)}, u32[]{:S(2)}) async-start(bf16[16,24,1280]{2,1,0:T(8,128)(2,1)} %bitcast.7), calls=%async_computation | async-start | bytes 1966080 | tf_op jit(solution)/shard_map/all_to_all | solution.py:248
  13.2 0.7 shard_map.103
  13.9 14.4 %all-to-all-done = bf16[16,24,1280]{2,1,0:T(8,128)(2,1)S(1)} async-done(((bf16[16,24,1280]{2,1,0:T(8,128)(2,1)}), bf16[16,24,1280]{2,1,0:T(8,128)(2,1)S(1)}, u32[]{:S(2)}, u32[]{:S(2)}) %all-to-all-start) | async-done | bytes 983072 | tf_op jit(solution)/shard_map/all_to_all | solution.py:248
  28.3 2.5 %collective-permute-start.1 = (bf16[384,1280]{1,0:T(8,128)(2,1)S(1)}, bf16[384,1280]{1,0:T(8,128)(2,1)S(1)}, u32[]{:S(2)}, u32[]{:S(2)}) collective-permute-start(bf16[384,1280]{1,0:T(8,128)(2,1)S(1)} %bitcast.35), channel_id=1, source_target_pairs={{0,3},{1,0},{2,1},{3,2},{4,7},{5,4},{6,5},{7,6},{8,11},{9,8},{10,9... | collective-permute-start | bytes 2949128 | tf_op jit(solution)/shard_map/ppermute | solution.py:16
  30.8 0.0 collective-permute-start
  30.8 18.4 %all_to_all.15 = bf16[16,24,1280]{2,1,0:T(8,128)(2,1)S(1)} all-to-all(bf16[16,24,1280]{2,1,0:T(8,128)(2,1)S(1)} %bitcast.43), channel_id=1, replica_groups=mesh['section'=2,'ep'=16,'edp'=4] {'ep'}, dimensions={0} | all-to-all | bytes 1966080 | tf_op jit(solution)/shard_map/all_to_all | solution.py:248
  49.2 1.8 %collective-permute-done.1.refs_4_.refs_2_ = bf16[384,1280]{1,0:T(8,128)(2,1)S(1)} collective-permute-done((bf16[384,1280]{1,0:T(8,128)(2,1)S(1)}, bf16[384,1280]{1,0:T(8,128)(2,1)S(1)}, u32[]{:S(2)}, u32[]{:S(2)}) %collective-permute-start.1) | collective-permute-done | bytes 983072 | tf_op jit(solution)/shard_map/ppermute | solution.py:16
  51.0 3.1 %collective-permute-done.refs_3_.refs_1_ = bf16[384,1280]{1,0:T(8,128)(2,1)S(1)} collective-permute-done((bf16[384,1280]{1,0:T(8,128)(2,1)S(1)}, bf16[384,1280]{1,0:T(8,128)(2,1)S(1)}, u32[]{:S(2)}, u32[]{:S(2)}) %collective-permute-start) | collective-permute-done | bytes 983072 | tf_op jit(solution)/shard_map/ppermute | solution.py:16
  54.1 0.4 collective-permute-start.3
  54.5 1.1 collective-permute-start.2
  55.6 2.6 %collective-permute-start.4 = (s32[6,384]{1,0:T(8,128)S(1)}, s32[6,384]{1,0:T(8,128)S(1)}, u32[]{:S(2)}, u32[]{:S(2)}) collective-permute-start(s32[6,384]{1,0:T(8,128)S(1)} %bitcast.45), channel_id=1, source_target_pairs={{0,64},{64,0},{1,65},{65,1},{2,66},{66,2},{3,67},{67,3},{4,68},{68... | collective-permute-start | bytes 27656 | tf_op jit(solution)/shard_map/ppermute | solution.py:16
  58.3 1.6 collective-permute-start.6
  59.9 0.0 collective-permute-start.5
  60.0 0.0 copy-start.3
  60.0 2.1 %copy-done.3 = bf16[1,1,5120,384]{3,2,1,0:T(8,128)(2,1)S(1)} copy-done((bf16[1,1,5120,384]{3,2,1,0:T(8,128)(2,1)S(1)}, bf16[1,1,5120,384]{3,2,1,0:T(8,128)(2,1)}, u32[]{:S(2)}) %copy-start.3) | copy-done | bytes 3932184
  62.1 3.5 %shard_map.104 = (f32[384,384]{1,0:T(8,128)S(1)}, f32[384,384]{1,0:T(8,128)S(1)}, bf16[384,384]{1,0:T(8,128)(2,1)S(1)}) custom-call(s32[1]{0:T(128)} %bitcast.1.refs_0_.me_ref, s32[6,384]{1,0:T(8,128)S(1)} %collective-permute-done.4.refs_1_, bf16[384,1280]{1,0:T(8,128)(2,1)S(1)} %bitcast.37, bf16[384,1280]{1,0:T(8,128)(2,1)S(1)} %collective-permute-done.refs_3_.refs_1_, ...), custom_call_target="tpu_custom_call" | custom-call | flops 4529848320 | tf_op jit(solution)/shard_map/pallas_call | solution.py:201
  65.6 9.7 %collective-permute-done.3.y2.refs_7_ = bf16[384,1280]{1,0:T(8,128)(2,1)S(1)} collective-permute-done((bf16[384,1280]{1,0:T(8,128)(2,1)S(1)}, bf16[384,1280]{1,0:T(8,128)(2,1)S(1)}, u32[]{:S(2)}, u32[]{:S(2)}) %collective-permute-start.3) | collective-permute-done | bytes 983072 | tf_op jit(solution)/shard_map/ppermute | solution.py:16
  75.3 1.6 collective-permute-done.2.y1.refs_6_
  77.0 0.4 collective-permute-start.8
  77.3 1.2 collective-permute-start.7
  78.5 1.7 shard_map.105.back_ref
  80.3 5.5 %collective-permute-done.6.x31.refs_4_ = bf16[384,640]{1,0:T(8,128)(2,1)S(1)} collective-permute-done((bf16[384,640]{1,0:T(8,128)(2,1)S(1)}, bf16[384,640]{1,0:T(8,128)(2,1)S(1)}, u32[]{:S(2)}, u32[]{:S(2)}) %collective-permute-start.6) | collective-permute-done | bytes 491552 | tf_op jit(solution)/shard_map/ppermute | solution.py:16
  85.8 1.6 collective-permute-done.5.x30.refs_3_
  87.4 8.9 %collective-permute-done.8.y31.refs_9_ = bf16[384,640]{1,0:T(8,128)(2,1)S(1)} collective-permute-done((bf16[384,640]{1,0:T(8,128)(2,1)S(1)}, bf16[384,640]{1,0:T(8,128)(2,1)S(1)}, u32[]{:S(2)}, u32[]{:S(2)}) %collective-permute-start.8) | collective-permute-done | bytes 491552 | tf_op jit(solution)/shard_map/ppermute | solution.py:16
  96.4 1.6 collective-permute-done.7.y30.refs_8_
  98.0 3.3 %shard_map.106 = (bf16[384,384]{1,0:T(8,128)(2,1)S(1)}, bf16[384,384]{1,0:T(8,128)(2,1)S(1)}, bf16[384,384]{1,0:T(8,128)(2,1)S(1)}, bf16[384,640]{1,0:T(8,128)(2,1)S(1)}, bf16[384,640]{1,0:T(8,128)(2,1)S(1)}) custom-call(s32[1]{0:T(128)} %bitcast.1.refs_0_.me_ref, bf16[384,640]{1,0:T(8,128)(2,1)S(1)} %collective-permute-done.5.x30.refs_3_, ...), custom_call_target="tpu_custom_call" | custom-call | flops 3774873600 | tf_op jit(solution)/shard_map/pallas_call | solution.py:201
  101.3 0.7 copy-done.21
  102.1 2.7 %collective-permute-start.13 = (bf16[384,640]{1,0:T(8,128)(2,1)S(1)}, bf16[384,640]{1,0:T(8,128)(2,1)S(1)}, u32[]{:S(2)}, u32[]{:S(2)}) collective-permute-start(bf16[384,640]{1,0:T(8,128)(2,1)S(1)} %get-tuple-element.65), channel_id=1, source_target_pairs={{0,3},{1,0},{2,1},{3,2},{4,7},{5,4},{6,5},{7,6},{8,11},{9,8},{10,9... | collective-permute-start | bytes 1474568 | tf_op jit(solution)/shard_map/ppermute | solution.py:16
  104.8 3.2 %shard_map.107 = (bf16[384,640]{1,0:T(8,128)(2,1)S(1)}, bf16[384,640]{1,0:T(8,128)(2,1)S(1)}, bf16[384,640]{1,0:T(8,128)(2,1)S(1)}, bf16[384,640]{1,0:T(8,128)(2,1)S(1)}, bf16[384,1280]{1,0:T(8,128)(2,1)S(1)}) custom-call(s32[1]{0:T(128)} %bitcast.1.refs_0_.me_ref, bf16[384,384]{1,0:T(8,128)(2,1)S(1)} %get-tuple-element.68.dg_ref.refs_10_, ...), custom_call_target="tpu_custom_call" | custom-call | flops 4529848320 | tf_op jit(solution)/shard_map/pallas_call | solution.py:201
  108.0 0.1 collective-permute-start.11
  108.1 2.7 %collective-permute-start.12 = (bf16[384,640]{1,0:T(8,128)(2,1)S(1)}, bf16[384,640]{1,0:T(8,128)(2,1)S(1)}, u32[]{:S(2)}, u32[]{:S(2)}) collective-permute-start(bf16[384,640]{1,0:T(8,128)(2,1)S(1)} %get-tuple-element.63), channel_id=1, source_target_pairs={{0,3},{1,0},{2,1},{3,2},{4,7},{5,4},{6,5},{7,6},{8,11},{9,8},{10,9... | collective-permute-start | bytes 1474568 | tf_op jit(solution)/shard_map/ppermute | solution.py:16
  110.8 2.3 %collective-permute-done.9 = bf16[384,640]{1,0:T(8,128)(2,1)S(1)} collective-permute-done((bf16[384,640]{1,0:T(8,128)(2,1)S(1)}, bf16[384,640]{1,0:T(8,128)(2,1)S(1)}, u32[]{:S(2)}, u32[]{:S(2)}) %collective-permute-start.9) | collective-permute-done | bytes 491552 | tf_op jit(solution)/shard_map/ppermute | solution.py:16
  113.0 0.1 add_convert_fusion.1
  113.1 0.1 collective-permute-start.10
  113.2 0.1 add_convert_fusion
  113.4 2.7 %collective-permute-start.14 = (bf16[384,640]{1,0:T(8,128)(2,1)S(1)}, bf16[384,640]{1,0:T(8,128)(2,1)S(1)}, u32[]{:S(2)}, u32[]{:S(2)}) collective-permute-start(bf16[384,640]{1,0:T(8,128)(2,1)S(1)} %add_convert_fusion), channel_id=1, source_target_pairs={{0,3},{1,0},{2,1},{3,2},{4,7},{5,4},{6,5},{7,6},{8,11},{9,8},{10,9... | collective-permute-start | bytes 1474568 | tf_op jit(solution)/shard_map/ppermute | solution.py:16
  116.1 7.5 %collective-permute-done.11.l1_ref = bf16[384,640]{1,0:T(8,128)(2,1)S(1)} collective-permute-done((bf16[384,640]{1,0:T(8,128)(2,1)S(1)}, bf16[384,640]{1,0:T(8,128)(2,1)S(1)}, u32[]{:S(2)}, u32[]{:S(2)}) %collective-permute-start.11) | collective-permute-done | bytes 491552 | tf_op jit(solution)/shard_map/ppermute | solution.py:16
  123.6 10.5 %collective-permute-done.10.l0_ref = bf16[384,640]{1,0:T(8,128)(2,1)S(1)} collective-permute-done((bf16[384,640]{1,0:T(8,128)(2,1)S(1)}, bf16[384,640]{1,0:T(8,128)(2,1)S(1)}, u32[]{:S(2)}, u32[]{:S(2)}) %collective-permute-start.10) | collective-permute-done | bytes 491552 | tf_op jit(solution)/shard_map/ppermute | solution.py:16
  134.1 0.4 shard_map.108
  134.5 1.3 copy-done
  135.8 11.2 %all-to-all-start.2 = ((bf16[32,24,1280]{2,1,0:T(8,128)(2,1)}), bf16[32,24,1280]{2,1,0:T(8,128)(2,1)S(1)}, u32[]{:S(2)}, u32[]{:S(2)}) async-start(bf16[32,24,1280]{2,1,0:T(8,128)(2,1)} %bitcast.26), calls=%async_computation.2 | async-start | bytes 3932160 | tf_op jit(solution)/shard_map/all_to_all | solution.py:336
  147.0 13.2 %shard_map.110 = (bf16[5120,384]{1,0:T(8,128)(2,1)}, bf16[5120,384]{1,0:T(8,128)(2,1)}, bf16[384,5120]{1,0:T(8,128)(2,1)}) custom-call(s32[1]{0:T(128)} %bitcast.1.refs_0_.me_ref, bf16[384,1280]{1,0:T(8,128)(2,1)} %bitcast.38, bf16[384,1280]{1,0:T(8,128)(2,1)} %copy-done.14, bf16[384,1280]{1,0:T(8,128)(2,1)} %copy-done.13, bf16[384,640]{1,0:T(8,128)(2,1)} %copy-done.8, ...), custom_call_target="tpu_custom_call" | custom-call | flops 9059696640 | tf_op jit(solution)/shard_map/pallas_call | solution.py:318
  160.2 13.7 %all-to-all-done.2 = bf16[32,24,1280]{2,1,0:T(8,128)(2,1)S(1)} async-done(((bf16[32,24,1280]{2,1,0:T(8,128)(2,1)}), bf16[32,24,1280]{2,1,0:T(8,128)(2,1)S(1)}, u32[]{:S(2)}, u32[]{:S(2)}) %all-to-all-start.2) | async-done | bytes 1966112 | tf_op jit(solution)/shard_map/all_to_all | solution.py:336
  173.9 1.7 shard_map.109
  (49 shorter events, 0.3 us)
Async XLA Ops:
  1.3 1.2 copy-start.17
  2.5 0.7 copy-start.22
  3.2 10.0 %copy-start.18 = (bf16[1,384,1280]{2,1,0:T(8,128)(2,1)S(1)}, bf16[1,384,1280]{2,1,0:T(8,128)(2,1)}, u32[]{:S(2)}) copy-start(bf16[1,384,1280]{2,1,0:T(8,128)(2,1)} %param.8) | copy-start | bytes 2949124
  5.4 22.9 %all-to-all-start = ((bf16[16,24,1280]{2,1,0:T(8,128)(2,1)}), bf16[16,24,1280]{2,1,0:T(8,128)(2,1)S(1)}, u32[]{:S(2)}, u32[]{:S(2)}) async-start(bf16[16,24,1280]{2,1,0:T(8,128)(2,1)} %bitcast.7), calls=%async_computation | async-start | bytes 1966080 | tf_op jit(solution)/shard_map/all_to_all | solution.py:248
  28.3 37.2 %copy-start.5 = (bf16[16,24,1280]{2,1,0:T(8,128)(2,1)}, bf16[16,24,1280]{2,1,0:T(8,128)(2,1)S(1)}, u32[]{:S(2)}) copy-start(bf16[16,24,1280]{2,1,0:T(8,128)(2,1)S(1)} %all-to-all-done) | copy-start | bytes 2949124
  28.3 31.6 %copy-start.2 = (bf16[1,1,5120,384]{3,2,1,0:T(8,128)(2,1)S(1)}, bf16[1,1,5120,384]{3,2,1,0:T(8,128)(2,1)}, u32[]{:S(2)}) copy-start(bf16[1,1,5120,384]{3,2,1,0:T(8,128)(2,1)} %param.11) | copy-start | bytes 11796484
  28.3 22.7 %collective-permute-start.1 = (bf16[384,1280]{1,0:T(8,128)(2,1)S(1)}, bf16[384,1280]{1,0:T(8,128)(2,1)S(1)}, u32[]{:S(2)}, u32[]{:S(2)}) collective-permute-start(bf16[384,1280]{1,0:T(8,128)(2,1)S(1)} %bitcast.35), channel_id=1, source_target_pairs={{0,3},{1,0},{2,1},{3,2},{4,7},{5,4},{6,5},{7,6},{8,11},{9,8},{10,9... | collective-permute-start | bytes 2949128 | tf_op jit(solution)/shard_map/ppermute | solution.py:16
  30.8 23.3 %collective-permute-start = (bf16[384,1280]{1,0:T(8,128)(2,1)S(1)}, bf16[384,1280]{1,0:T(8,128)(2,1)S(1)}, u32[]{:S(2)}, u32[]{:S(2)}) collective-permute-start(bf16[384,1280]{1,0:T(8,128)(2,1)S(1)} %bitcast.36), channel_id=1, source_target_pairs={{0,1},{1,2},{2,3},{3,0},{4,5},{5,6},{6,7},{7,4},{8,9},{9,10},{10,1... | collective-permute-start | bytes 2949128 | tf_op jit(solution)/shard_map/ppermute | solution.py:16
  49.2 29.3 %copy-start.6 = (bf16[16,24,1280]{2,1,0:T(8,128)(2,1)}, bf16[16,24,1280]{2,1,0:T(8,128)(2,1)S(1)}, u32[]{:S(2)}) copy-start(bf16[16,24,1280]{2,1,0:T(8,128)(2,1)S(1)} %all_to_all.15) | copy-start | bytes 2949124
  51.0 14.6 %copy-start.13 = (bf16[384,1280]{1,0:T(8,128)(2,1)}, bf16[384,1280]{1,0:T(8,128)(2,1)S(1)}, u32[]{:S(2)}) copy-start(bf16[384,1280]{1,0:T(8,128)(2,1)S(1)} %collective-permute-done.1.refs_4_.refs_2_) | copy-start | bytes 2949124
  54.1 11.5 %copy-start.14 = (bf16[384,1280]{1,0:T(8,128)(2,1)}, bf16[384,1280]{1,0:T(8,128)(2,1)S(1)}, u32[]{:S(2)}) copy-start(bf16[384,1280]{1,0:T(8,128)(2,1)S(1)} %collective-permute-done.refs_3_.refs_1_) | copy-start | bytes 2949124
  54.1 21.2 %collective-permute-start.3 = (bf16[384,1280]{1,0:T(8,128)(2,1)S(1)}, bf16[384,1280]{1,0:T(8,128)(2,1)S(1)}, u32[]{:S(2)}, u32[]{:S(2)}) collective-permute-start(bf16[384,1280]{1,0:T(8,128)(2,1)S(1)} %bitcast.39), channel_id=1, source_target_pairs={{0,3},{1,0},{2,1},{3,2},{4,7},{5,4},{6,5},{7,6},{8,11},{9,8},{10,9... | collective-permute-start | bytes 2949128 | tf_op jit(solution)/shard_map/ppermute | solution.py:16
  54.5 22.4 %collective-permute-start.2 = (bf16[384,1280]{1,0:T(8,128)(2,1)S(1)}, bf16[384,1280]{1,0:T(8,128)(2,1)S(1)}, u32[]{:S(2)}, u32[]{:S(2)}) collective-permute-start(bf16[384,1280]{1,0:T(8,128)(2,1)S(1)} %bitcast.40), channel_id=1, source_target_pairs={{0,1},{1,2},{2,3},{3,0},{4,5},{5,6},{6,7},{7,4},{8,9},{9,10},{10,1... | collective-permute-start | bytes 2949128 | tf_op jit(solution)/shard_map/ppermute | solution.py:16
  55.6 4.4 %collective-permute-start.4 = (s32[6,384]{1,0:T(8,128)S(1)}, s32[6,384]{1,0:T(8,128)S(1)}, u32[]{:S(2)}, u32[]{:S(2)}) collective-permute-start(s32[6,384]{1,0:T(8,128)S(1)} %bitcast.45), channel_id=1, source_target_pairs={{0,64},{64,0},{1,65},{65,1},{2,66},{66,2},{3,67},{67,3},{4,68},{68... | collective-permute-start | bytes 27656 | tf_op jit(solution)/shard_map/ppermute | solution.py:16
  58.3 27.5 %collective-permute-start.6 = (bf16[384,640]{1,0:T(8,128)(2,1)S(1)}, bf16[384,640]{1,0:T(8,128)(2,1)S(1)}, u32[]{:S(2)}, u32[]{:S(2)}) collective-permute-start(bf16[384,640]{1,0:T(8,128)(2,1)S(1)} %slice.13), channel_id=1, source_target_pairs={{0,3},{1,0},{2,1},{3,2},{4,7},{5,4},{6,5},{7,6},{8,11},{9,8},{10,9... | collective-permute-start | bytes 1474568 | tf_op jit(solution)/shard_map/ppermute | solution.py:16
  59.9 27.5 %collective-permute-start.5 = (bf16[384,640]{1,0:T(8,128)(2,1)S(1)}, bf16[384,640]{1,0:T(8,128)(2,1)S(1)}, u32[]{:S(2)}, u32[]{:S(2)}) collective-permute-start(bf16[384,640]{1,0:T(8,128)(2,1)S(1)} %slice.12), channel_id=1, source_target_pairs={{0,1},{1,2},{2,3},{3,0},{4,5},{5,6},{6,7},{7,4},{8,9},{9,10},{10,1... | collective-permute-start | bytes 1474568 | tf_op jit(solution)/shard_map/ppermute | solution.py:16
  60.0 2.1 %copy-start.3 = (bf16[1,1,5120,384]{3,2,1,0:T(8,128)(2,1)S(1)}, bf16[1,1,5120,384]{3,2,1,0:T(8,128)(2,1)}, u32[]{:S(2)}) copy-start(bf16[1,1,5120,384]{3,2,1,0:T(8,128)(2,1)} %param.12) | copy-start | bytes 11796484
  62.1 16.5 %copy-start.1 = (bf16[1,1,384,5120]{3,2,1,0:T(8,128)(2,1)S(1)}, bf16[1,1,384,5120]{3,2,1,0:T(8,128)(2,1)}, u32[]{:S(2)}) copy-start(bf16[1,1,384,5120]{3,2,1,0:T(8,128)(2,1)} %param.13) | copy-start | bytes 11796484
  65.6 14.7 %copy-start.11 = (bf16[384,384]{1,0:T(8,128)(2,1)}, bf16[384,384]{1,0:T(8,128)(2,1)S(1)}, u32[]{:S(2)}) copy-start(bf16[384,384]{1,0:T(8,128)(2,1)S(1)} %get-tuple-element.52.choice_ref) | copy-start | bytes 884740
  75.3 5.0 %copy-start.15 = (bf16[384,1280]{1,0:T(8,128)(2,1)}, bf16[384,1280]{1,0:T(8,128)(2,1)S(1)}, u32[]{:S(2)}) copy-start(bf16[384,1280]{1,0:T(8,128)(2,1)S(1)} %collective-permute-done.3.y2.refs_7_) | copy-start | bytes 2949124
  76.9 3.4 %copy-start.16 = (bf16[384,1280]{1,0:T(8,128)(2,1)}, bf16[384,1280]{1,0:T(8,128)(2,1)S(1)}, u32[]{:S(2)}) copy-start(bf16[384,1280]{1,0:T(8,128)(2,1)S(1)} %collective-permute-done.2.y1.refs_6_) | copy-start | bytes 2949124
  77.0 19.4 %collective-permute-start.8 = (bf16[384,640]{1,0:T(8,128)(2,1)S(1)}, bf16[384,640]{1,0:T(8,128)(2,1)S(1)}, u32[]{:S(2)}, u32[]{:S(2)}) collective-permute-start(bf16[384,640]{1,0:T(8,128)(2,1)S(1)} %slice.15), channel_id=1, source_target_pairs={{0,3},{1,0},{2,1},{3,2},{4,7},{5,4},{6,5},{7,6},{8,11},{9,8},{10,9... | collective-permute-start | bytes 1474568 | tf_op jit(solution)/shard_map/ppermute | solution.py:16
  77.3 20.6 %collective-permute-start.7 = (bf16[384,640]{1,0:T(8,128)(2,1)S(1)}, bf16[384,640]{1,0:T(8,128)(2,1)S(1)}, u32[]{:S(2)}, u32[]{:S(2)}) collective-permute-start(bf16[384,640]{1,0:T(8,128)(2,1)S(1)} %slice.14), channel_id=1, source_target_pairs={{0,1},{1,2},{2,3},{3,0},{4,5},{5,6},{6,7},{7,4},{8,9},{9,10},{10,1... | collective-permute-start | bytes 1474568 | tf_op jit(solution)/shard_map/ppermute | solution.py:16
  78.5 19.4 %copy-start.4 = (bf16[1,1,5120,384]{3,2,1,0:T(8,128)(2,1)S(1)}, bf16[1,1,5120,384]{3,2,1,0:T(8,128)(2,1)}, u32[]{:S(2)}) copy-start(bf16[1,1,5120,384]{3,2,1,0:T(8,128)(2,1)} %param.12) | copy-start | bytes 11796484
  85.8 15.5 %copy-start.7 = (bf16[384,640]{1,0:T(8,128)(2,1)}, bf16[384,640]{1,0:T(8,128)(2,1)S(1)}, u32[]{:S(2)}) copy-start(bf16[384,640]{1,0:T(8,128)(2,1)S(1)} %collective-permute-done.6.x31.refs_4_) | copy-start | bytes 1474564
  87.4 13.9 %copy-start.8 = (bf16[384,640]{1,0:T(8,128)(2,1)}, bf16[384,640]{1,0:T(8,128)(2,1)S(1)}, u32[]{:S(2)}) copy-start(bf16[384,640]{1,0:T(8,128)(2,1)S(1)} %collective-permute-done.5.x30.refs_3_) | copy-start | bytes 1474564
  96.3 5.0 %copy-start.9 = (bf16[384,640]{1,0:T(8,128)(2,1)}, bf16[384,640]{1,0:T(8,128)(2,1)S(1)}, u32[]{:S(2)}) copy-start(bf16[384,640]{1,0:T(8,128)(2,1)S(1)} %collective-permute-done.8.y31.refs_9_) | copy-start | bytes 1474564
  98.0 3.4 %copy-start.10 = (bf16[384,640]{1,0:T(8,128)(2,1)}, bf16[384,640]{1,0:T(8,128)(2,1)S(1)}, u32[]{:S(2)}) copy-start(bf16[384,640]{1,0:T(8,128)(2,1)S(1)} %collective-permute-done.7.y30.refs_8_) | copy-start | bytes 1474564
  101.3 0.7 copy-start.21
  102.1 5.9 %copy-start.19 = (bf16[384,384]{1,0:T(8,128)(2,1)}, bf16[384,384]{1,0:T(8,128)(2,1)S(1)}, u32[]{:S(2)}) copy-start(bf16[384,384]{1,0:T(8,128)(2,1)S(1)} %get-tuple-element.68.dg_ref.refs_10_) | copy-start | bytes 884740
  102.1 5.9 %copy-start.20 = (bf16[384,384]{1,0:T(8,128)(2,1)}, bf16[384,384]{1,0:T(8,128)(2,1)S(1)}, u32[]{:S(2)}) copy-start(bf16[384,384]{1,0:T(8,128)(2,1)S(1)} %get-tuple-element.69.du_ref.refs_11_) | copy-start | bytes 884740
  102.1 11.0 %collective-permute-start.9 = (bf16[384,640]{1,0:T(8,128)(2,1)S(1)}, bf16[384,640]{1,0:T(8,128)(2,1)S(1)}, u32[]{:S(2)}, u32[]{:S(2)}) collective-permute-start(bf16[384,640]{1,0:T(8,128)(2,1)S(1)} %get-tuple-element.61), channel_id=1, source_target_pairs={{0,1},{1,2},{2,3},{3,0},{4,5},{5,6},{6,7},{7,4},{8,9},{9,10},{10,1... | collective-permute-start | bytes 1474568 | tf_op jit(solution)/shard_map/ppermute | solution.py:16
  102.1 11.2 %collective-permute-start.13 = (bf16[384,640]{1,0:T(8,128)(2,1)S(1)}, bf16[384,640]{1,0:T(8,128)(2,1)S(1)}, u32[]{:S(2)}, u32[]{:S(2)}) collective-permute-start(bf16[384,640]{1,0:T(8,128)(2,1)S(1)} %get-tuple-element.65), channel_id=1, source_target_pairs={{0,3},{1,0},{2,1},{3,2},{4,7},{5,4},{6,5},{7,6},{8,11},{9,8},{10,9... | collective-permute-start | bytes 1474568 | tf_op jit(solution)/shard_map/ppermute | solution.py:16
  108.0 15.6 %collective-permute-start.11 = (bf16[384,640]{1,0:T(8,128)(2,1)S(1)}, bf16[384,640]{1,0:T(8,128)(2,1)S(1)}, u32[]{:S(2)}, u32[]{:S(2)}) collective-permute-start(bf16[384,640]{1,0:T(8,128)(2,1)S(1)} %get-tuple-element.62), channel_id=1, source_target_pairs={{0,1},{1,2},{2,3},{3,0},{4,5},{5,6},{6,7},{7,4},{8,9},{9,10},{10,1... | collective-permute-start | bytes 1474568 | tf_op jit(solution)/shard_map/ppermute | solution.py:16
  108.1 15.5 %collective-permute-start.12 = (bf16[384,640]{1,0:T(8,128)(2,1)S(1)}, bf16[384,640]{1,0:T(8,128)(2,1)S(1)}, u32[]{:S(2)}, u32[]{:S(2)}) collective-permute-start(bf16[384,640]{1,0:T(8,128)(2,1)S(1)} %get-tuple-element.63), channel_id=1, source_target_pairs={{0,3},{1,0},{2,1},{3,2},{4,7},{5,4},{6,5},{7,6},{8,11},{9,8},{10,9... | collective-permute-start | bytes 1474568 | tf_op jit(solution)/shard_map/ppermute | solution.py:16
  113.1 20.9 %collective-permute-start.10 = (bf16[384,640]{1,0:T(8,128)(2,1)S(1)}, bf16[384,640]{1,0:T(8,128)(2,1)S(1)}, u32[]{:S(2)}, u32[]{:S(2)}) collective-permute-start(bf16[384,640]{1,0:T(8,128)(2,1)S(1)} %add_convert_fusion.1), channel_id=1, source_target_pairs={{0,1},{1,2},{2,3},{3,0},{4,5},{5,6},{6,7},{7,4},{8,9},{9,10},{10,1... | collective-permute-start | bytes 1474568 | tf_op jit(solution)/shard_map/ppermute | solution.py:16
  113.4 20.7 %collective-permute-start.14 = (bf16[384,640]{1,0:T(8,128)(2,1)S(1)}, bf16[384,640]{1,0:T(8,128)(2,1)S(1)}, u32[]{:S(2)}, u32[]{:S(2)}) collective-permute-start(bf16[384,640]{1,0:T(8,128)(2,1)S(1)} %add_convert_fusion), channel_id=1, source_target_pairs={{0,3},{1,0},{2,1},{3,2},{4,7},{5,4},{6,5},{7,6},{8,11},{9,8},{10,9... | collective-permute-start | bytes 1474568 | tf_op jit(solution)/shard_map/ppermute | solution.py:16
  134.5 1.3 copy-start
  135.8 38.1 %all-to-all-start.2 = ((bf16[32,24,1280]{2,1,0:T(8,128)(2,1)}), bf16[32,24,1280]{2,1,0:T(8,128)(2,1)S(1)}, u32[]{:S(2)}, u32[]{:S(2)}) async-start(bf16[32,24,1280]{2,1,0:T(8,128)(2,1)} %bitcast.26), calls=%async_computation.2 | async-start | bytes 3932160 | tf_op jit(solution)/shard_map/all_to_all | solution.py:336
  147.0 26.9 %copy-start.12 = (bf16[384,384]{1,0:T(8,128)(2,1)S(1)}, bf16[384,384]{1,0:T(8,128)(2,1)}, u32[]{:S(2)}) copy-start(bf16[384,384]{1,0:T(8,128)(2,1)} %copy-done.11) | copy-start | bytes 884740

commit v3 on v2

--- a/solution.py
+++ b/solution.py
@@ -120,8 +120,7 @@
     dg_ref[...] = dg
     du_ref[...] = du
     gh_ref[...] = (swish * up_pre).astype(jnp.bfloat16)
-    for h, p_ref in enumerate((p0_ref, p1_ref)):
-        rows = slice(h * half, (h + 1) * half)
+    for p_ref, rows in ((p0_ref, slice(0, SHIFTED)), (p1_ref, slice(SHIFTED, width))):
         p_ref[...] = (contract(dg, wg[rows], 1, 1) + contract(du, wu[rows], 1, 1)).astype(
             jnp.bfloat16
         )
@@ -129,8 +128,7 @@
 
 def part_kernel(me_ref, dg_ref, du_ref, wg_ref, wu_ref, r0_ref, r1_ref, l0_ref, l1_ref, own_ref):
     width = own_ref.shape[1]
-    half = width // 2
-    for offset, outs in ((1, (r0_ref, r1_ref)), (3, (l0_ref, l1_ref)), (0, (own_ref,))):
+    for offset, outs in ((3, (l0_ref, l1_ref)), (1, (r0_ref, r1_ref)), (0, (own_ref,))):
         at = lax.rem(me_ref[0] + offset, 4)
         wg = rows_at(wg_ref, at, width)
         wu = rows_at(wu_ref, at, width)
@@ -139,20 +137,27 @@
         if len(outs) == 1:
             own_ref[...] = part
         else:
-            outs[0][...] = part[:, :half]
-            outs[1][...] = part[:, half:]
-
-
-def sum_kernel(own_ref, l0_ref, l1_ref, r0_ref, r1_ref, out_ref):
-    half = l0_ref.shape[1]
+            outs[0][...] = part[:, :SHIFTED]
+            outs[1][...] = part[:, SHIFTED:]
+
+
+def sum_kernel(own_ref, l_ref, r_ref, out_ref):
+    total = own_ref[:, :SHIFTED].astype(jnp.float32)
+    total = total + l_ref[...].astype(jnp.float32) + r_ref[...].astype(jnp.float32)
+    out_ref[...] = total.astype(jnp.bfloat16)
+
+
+def pack_kernel(section_ref, own_ref, l_ref, r_ref, shifted_ref, out_ref):
     rows = own_ref.shape[0]
-    for h, (a, b) in enumerate(((l0_ref, r0_ref), (l1_ref, r1_ref))):
-        columns = slice(h * half, (h + 1) * half)
-        total = own_ref[:, columns].astype(jnp.float32)
-        total = total + a[...].astype(jnp.float32) + b[...].astype(jnp.float32)
-        total = total.astype(jnp.bfloat16)
-        out_ref[:rows, columns] = total
-        out_ref[rows:, columns] = total
+    here = pl.multiple_of(section_ref[0] * rows, 128)
+    there = pl.multiple_of((1 - section_ref[0]) * rows, 128)
+    total = own_ref[:, SHIFTED:].astype(jnp.float32)
+    total = total + l_ref[...].astype(jnp.float32) + r_ref[...].astype(jnp.float32)
+    out_ref[pl.ds(there, rows), :] = total.astype(jnp.bfloat16)
+    out_ref[pl.ds(here, rows), :SHIFTED] = shifted_ref[...]
+    unused = out_ref.shape[1] - SHIFTED
+    if unused:
+        out_ref[pl.ds(here, rows), SHIFTED:] = jnp.zeros((rows, unused), jnp.bfloat16)
 
 
 def grad_kernel(me_ref, *refs):
@@ -171,10 +176,12 @@
                 out_d[:, span] = contract(gh[...], y_ref[...], 0, 0).astype(jnp.bfloat16)
 
 
-def combine_kernel(other_ref, choice_ref, rows_ref, out_ref):
+def combine_kernel(section_ref, choice_ref, rows_ref, out_ref):
     slots = choice_ref.shape[0]
-    rows = rows_at(rows_ref, other_ref[0], slots)
-    out_ref[...] = contract(choice_ref[...], rows, 0, 0).astype(jnp.bfloat16)
+    shifted = rows_at(rows_ref, section_ref[0], slots)[:, :SHIFTED]
+    out_ref[:, :SHIFTED] = contract(choice_ref[...], shifted, 0, 0).astype(jnp.bfloat16)
+    rest = rows_at(rows_ref, 1 - section_ref[0], slots)
+    out_ref[:, SHIFTED:] = contract(choice_ref[...], rest, 0, 0).astype(jnp.bfloat16)
 
 
 def bf16(*shape):
@@ -208,6 +215,7 @@
     )(*scalars, *arrays)
 
 
+SHIFTED = 512
 ORDER = (0, 3, 1, 2)
 
 
@@ -227,9 +235,9 @@
     one_slice = rows * width * hidden
     w_gate, w_up, w_down = w_gate[0, 0], w_up[0, 0], w_down[0, 0]
     me = lax.axis_index("edp").astype(jnp.int32).reshape(1)
-    other = (1 - lax.axis_index("section")).astype(jnp.int32).reshape(1)
-
-    routes, me, other = lax.optimization_barrier((routes[0].T, me, other))
+    section = lax.axis_index("section").astype(jnp.int32).reshape(1)
+
+    routes, me, section = lax.optimization_barrier((routes[0].T, me, section))
     next_routes = passed_along(routes, "section", -1)
 
     send_x, gated = call(
@@ -278,9 +286,10 @@
         (own_y, y_left, y_right, w_down),
         3 * one_slice,
     )
+    parts = [bf16(rows, SHIFTED), bf16(rows, width - SHIFTED)]
     d_gate, d_up, gated_hidden, far0, far1 = call(
         mid_kernel,
-        [bf16(rows, hidden)] * 3 + [bf16(rows, half)] * 2,
+        [bf16(rows, hidden)] * 3 + parts,
         (me,),
         (x_far0, x_far1, y_far0, y_far1, gate_pre, up_pre, back, w_gate, w_up, w_down),
         5 * one_slice,
@@ -289,7 +298,7 @@
     far1 = passed_along(far1, "edp", -1)
     right0, right1, left0, left1, own = call(
         part_kernel,
-        [bf16(rows, half)] * 4 + [bf16(rows, width)],
+        parts * 2 + [bf16(rows, width)],
         (me,),
         (d_gate, d_up, w_gate, w_up),
         6 * one_slice,
@@ -298,19 +307,21 @@
     def added(a, b):
         return (a.astype(jnp.float32) + b.astype(jnp.float32)).astype(jnp.bfloat16)
 
+    right0, right1 = lax.optimization_barrier((added(right0, far0), right1))
+    from_left0 = passed_along(right0, "edp", 1)
+    from_right0 = passed_along(left0, "edp", -1)
     from_left1 = passed_along(right1, "edp", 1)
-    from_right0 = passed_along(left0, "edp", -1)
-    from_left0 = passed_along(added(right0, far0), "edp", 1)
     from_right1 = passed_along(added(left1, far1), "edp", -1)
-
-    (summed,) = call(
-        sum_kernel,
-        [bf16(2 * rows, width)],
-        (),
-        (own, from_left0, from_left1, from_right0, from_right1),
-    )
-    summed, d_gate, d_up, gated_hidden = lax.optimization_barrier(
-        (summed, d_gate, d_up, gated_hidden)
+    (shifted,) = call(sum_kernel, parts[:1], (), (own, from_left0, from_right0))
+    shifted = passed_along(shifted, "section", -1)
+    (packed,) = call(
+        pack_kernel,
+        [bf16(2 * rows, max(SHIFTED, width - SHIFTED))],
+        (section,),
+        (own, from_left1, from_right1, shifted),
+    )
+    packed, d_gate, d_up, gated_hidden = lax.optimization_barrier(
+        (packed, d_gate, d_up, gated_hidden)
     )
     x = (own_x, x_left, x_right, x_far0, x_far1)
     y = (own_y, y_left, y_right, y_far0, y_far1)
@@ -334,16 +345,16 @@
         ),
     )(me, *(in_hbm(a) for a in (*x, *y, *smalls)))
     returned = lax.all_to_all(
-        summed.reshape(2 * ep_count, CAP, width),
+        packed.reshape(2 * ep_count, CAP, -1),
         ("section", "ep"),
         split_axis=0,
         concat_axis=0,
         tiled=True,
-    ).reshape(2 * rows, width)
+    ).reshape(2 * rows, -1)
     (grad_prev,) = call(
         combine_kernel,
         [bf16(token_count, width)],
-        (other,),
+        (section,),
         (choice, returned),
         rows * token_count * width,
     )

time: 176 us -> 168 us (0.955)
  waiting for transfers between devices: 82.3 us -> 73.8 us
  local copies, waits for them, and re-layouts: 6.99 us -> 4.94 us
    all_to_all x1, waiting for transfers between devices: 13.7 us -> 5.18 us  [body(): lax.all_to_all(packed.reshape(2 * ep_count, CAP, -1), ('section', 'ep'),...]
    unnamed x47 -> x41, local copies, waits for them, and re-layouts: 6.82 us -> 4.77 us
    ppermute x15 -> x16, starting transfers between devices: 18 us -> 19.1 us  [passed_along(): lax.ppermute(array, axis, [(i, (i + by) % length) for i in range(length)])]
    pallas_call x8 -> x9, Pallas kernels: 16.6 us -> 17.5 us  [call(): pl.pallas_call(kernel, out_shape=outs, in_specs=[IN_SMEM] * len(scalars)...]
    ppermute x15 -> x16, waiting for transfers between devices: 54.2 us -> 54.2 us  [passed_along(): lax.ppermute(array, axis, [(i, (i + by) % length) for i in range(length)])]
  transfers between devices with their start and end apart: 17 -> 18, of which waited for: 13 -> 15; matrix products, arithmetic and copies ran while one was open for 0% -> 0% of each run, Pallas kernels for 13% -> 13%
where the time goes in v3:
time: 168 us; the launch traced here: 167 us
  waiting for transfers between devices  73.8 us (44%)
  starting transfers between devices  38.4 us (23%)
  Pallas kernels  30.7 us (18%)
  blocking collectives  18.4 us (11%)
  local copies, waits for them, and re-layouts  4.94 us (3%)
    ppermute x16, waiting for transfers between devices, passed_along(): lax.ppermute(array, axis, [(i, (i + by) % length) for i in range(length)])  54.2 us
    ppermute x16, starting transfers between devices, passed_along(): lax.ppermute(array, axis, [(i, (i + by) % length) for i in range(length)])  19.1 us
    all_to_all x1, blocking collectives, to_experts(): lax.all_to_all(shaped, 'ep', split_axis=0, concat_axis=0, tiled=True)  18.4 us
    pallas_call x9, Pallas kernels, call(): pl.pallas_call(kernel, out_shape=outs, in_specs=[IN_SMEM] * len(scalars)...  17.5 us
    all_to_all x1, waiting for transfers between devices, to_experts(): lax.all_to_all(shaped, 'ep', split_axis=0, concat_axis=0, tiled=True)  14.4 us
    pallas_call x1, Pallas kernels, body(): pl.pallas_call(grad_kernel, out_shape=[bf16(4 * width, hidden)] * 2 + [bf...  13.2 us
    all_to_all x1, starting transfers between devices, body(): lax.all_to_all(packed.reshape(2 * ep_count, CAP, -1), ('section', 'ep'),...  11.5 us
    all_to_all x1, starting transfers between devices, to_experts(): lax.all_to_all(shaped, 'ep', split_axis=0, concat_axis=0, tiled=True)  7.84 us
  transfers between devices with their start and end apart: 18, of which 15 were waited for; matrix products, arithmetic and copies ran while one was open for 0% of the time, Pallas kernels for 13%

profile of v3, /device:TPU:1, one launch (start us, length us, event | category | flops | bytes accessed | tf_op | source)
XLA Modules:
  0.0 167.4 jit_solution(15117345781347399710)
XLA Ops:
  0.6 0.7 copy.13
  1.3 1.2 copy-done.14
  2.5 0.7 copy-done.19
  3.2 2.2 %shard_map.102 = (bf16[384,1280]{1,0:T(8,128)(2,1)}, bf16[384,384]{1,0:T(8,128)(2,1)S(1)}) custom-call(s32[6,384]{1,0:T(8,128)S(1)} %bitcast.43, bf16[6,384]{1,0:T(8,128)(2,1)S(1)} %bitcast.47, bf16[384,1280]{1,0:T(8,128)(2,1)S(1)} %bitcast.45), custom_call_target="tpu_custom_call" | custom-call | flops 981467136 | tf_op jit(solution)/shard_map/pallas_call | solution.py:208
  5.4 7.8 %all-to-all-start = ((bf16[16,24,1280]{2,1,0:T(8,128)(2,1)}), bf16[16,24,1280]{2,1,0:T(8,128)(2,1)S(1)}, u32[]{:S(2)}, u32[]{:S(2)}) async-start(bf16[16,24,1280]{2,1,0:T(8,128)(2,1)} %bitcast.7), calls=%async_computation | async-start | bytes 1966080 | tf_op jit(solution)/shard_map/all_to_all | solution.py:256
  13.2 0.7 shard_map.103
  13.9 14.4 %all-to-all-done = bf16[16,24,1280]{2,1,0:T(8,128)(2,1)S(1)} async-done(((bf16[16,24,1280]{2,1,0:T(8,128)(2,1)}), bf16[16,24,1280]{2,1,0:T(8,128)(2,1)S(1)}, u32[]{:S(2)}, u32[]{:S(2)}) %all-to-all-start) | async-done | bytes 983072 | tf_op jit(solution)/shard_map/all_to_all | solution.py:256
  28.3 2.5 %collective-permute-start.1 = (bf16[384,1280]{1,0:T(8,128)(2,1)S(1)}, bf16[384,1280]{1,0:T(8,128)(2,1)S(1)}, u32[]{:S(2)}, u32[]{:S(2)}) collective-permute-start(bf16[384,1280]{1,0:T(8,128)(2,1)S(1)} %bitcast.34), channel_id=1, source_target_pairs={{0,3},{1,0},{2,1},{3,2},{4,7},{5,4},{6,5},{7,6},{8,11},{9,8},{10,9... | collective-permute-start | bytes 2949128 | tf_op jit(solution)/shard_map/ppermute | solution.py:16
  30.8 18.4 %all_to_all.15 = bf16[16,24,1280]{2,1,0:T(8,128)(2,1)S(1)} all-to-all(bf16[16,24,1280]{2,1,0:T(8,128)(2,1)S(1)} %bitcast.42), channel_id=1, replica_groups=mesh['section'=2,'ep'=16,'edp'=4] {'ep'}, dimensions={0} | all-to-all | bytes 1966080 | tf_op jit(solution)/shard_map/all_to_all | solution.py:256
  49.2 1.8 %collective-permute-done.1.refs_4_.refs_2_ = bf16[384,1280]{1,0:T(8,128)(2,1)S(1)} collective-permute-done((bf16[384,1280]{1,0:T(8,128)(2,1)S(1)}, bf16[384,1280]{1,0:T(8,128)(2,1)S(1)}, u32[]{:S(2)}, u32[]{:S(2)}) %collective-permute-start.1) | collective-permute-done | bytes 983072 | tf_op jit(solution)/shard_map/ppermute | solution.py:16
  51.0 3.1 %collective-permute-done.refs_3_.refs_1_ = bf16[384,1280]{1,0:T(8,128)(2,1)S(1)} collective-permute-done((bf16[384,1280]{1,0:T(8,128)(2,1)S(1)}, bf16[384,1280]{1,0:T(8,128)(2,1)S(1)}, u32[]{:S(2)}, u32[]{:S(2)}) %collective-permute-start) | collective-permute-done | bytes 983072 | tf_op jit(solution)/shard_map/ppermute | solution.py:16
  54.1 0.4 collective-permute-start.3
  54.5 1.1 collective-permute-start.2
  55.6 2.6 %collective-permute-start.4 = (s32[6,384]{1,0:T(8,128)S(1)}, s32[6,384]{1,0:T(8,128)S(1)}, u32[]{:S(2)}, u32[]{:S(2)}) collective-permute-start(s32[6,384]{1,0:T(8,128)S(1)} %bitcast.44), channel_id=1, source_target_pairs={{0,64},{64,0},{1,65},{65,1},{2,66},{66,2},{3,67},{67,3},{4,68},{68... | collective-permute-start | bytes 27656 | tf_op jit(solution)/shard_map/ppermute | solution.py:16
  58.3 1.6 collective-permute-start.6
  60.0 2.1 %copy-done.2 = bf16[1,1,5120,384]{3,2,1,0:T(8,128)(2,1)S(1)} copy-done((bf16[1,1,5120,384]{3,2,1,0:T(8,128)(2,1)S(1)}, bf16[1,1,5120,384]{3,2,1,0:T(8,128)(2,1)}, u32[]{:S(2)}) %copy-start.2) | copy-done | bytes 3932184
  62.1 3.5 %shard_map.104 = (f32[384,384]{1,0:T(8,128)S(1)}, f32[384,384]{1,0:T(8,128)S(1)}, bf16[384,384]{1,0:T(8,128)(2,1)S(1)}) custom-call(s32[1]{0:T(128)} %bitcast.1.refs_0_.me_ref, s32[6,384]{1,0:T(8,128)S(1)} %collective-permute-done.4.refs_1_, bf16[384,1280]{1,0:T(8,128)(2,1)S(1)} %bitcast.36, bf16[384,1280]{1,0:T(8,128)(2,1)S(1)} %collective-permute-done.refs_3_.refs_1_, ...), custom_call_target="tpu_custom_call" | custom-call | flops 4529848320 | tf_op jit(solution)/shard_map/pallas_call | solution.py:208
  65.6 9.7 %collective-permute-done.3.y2.refs_7_ = bf16[384,1280]{1,0:T(8,128)(2,1)S(1)} collective-permute-done((bf16[384,1280]{1,0:T(8,128)(2,1)S(1)}, bf16[384,1280]{1,0:T(8,128)(2,1)S(1)}, u32[]{:S(2)}, u32[]{:S(2)}) %collective-permute-start.3) | collective-permute-done | bytes 983072 | tf_op jit(solution)/shard_map/ppermute | solution.py:16
  75.3 1.6 collective-permute-done.2.y1.refs_6_
  77.0 0.4 collective-permute-start.8
  77.4 1.2 collective-permute-start.7
  78.5 1.7 %shard_map.105.back_ref = f32[384,384]{1,0:T(8,128)S(1)} custom-call(s32[1]{0:T(128)} %bitcast.1.refs_0_.me_ref, bf16[384,1280]{1,0:T(8,128)(2,1)S(1)} %bitcast.40, bf16[384,1280]{1,0:T(8,128)(2,1)S(1)} %collective-permute-done.2.y1.refs_6_, bf16[384,1280]{1,0:T(8,128)(2,1)S(1)} %collective-permute-done.3.y2.refs_7_, bf16[384,5120]{1,0:T(8,128)(2,1)S(1)} %bitcast.25), custom_call_target="tpu_custom_call" | custom-call | flops 2264924160 | tf_op jit(solution)/shard_map/pallas_call | solution.py:208
  80.3 5.6 %collective-permute-done.6.x31.refs_4_ = bf16[384,640]{1,0:T(8,128)(2,1)S(1)} collective-permute-done((bf16[384,640]{1,0:T(8,128)(2,1)S(1)}, bf16[384,640]{1,0:T(8,128)(2,1)S(1)}, u32[]{:S(2)}, u32[]{:S(2)}) %collective-permute-start.6) | collective-permute-done | bytes 491552 | tf_op jit(solution)/shard_map/ppermute | solution.py:16
  85.8 1.6 collective-permute-done.5.x30.refs_3_
  87.4 8.9 %collective-permute-done.8.y31.refs_9_ = bf16[384,640]{1,0:T(8,128)(2,1)S(1)} collective-permute-done((bf16[384,640]{1,0:T(8,128)(2,1)S(1)}, bf16[384,640]{1,0:T(8,128)(2,1)S(1)}, u32[]{:S(2)}, u32[]{:S(2)}) %collective-permute-start.8) | collective-permute-done | bytes 491552 | tf_op jit(solution)/shard_map/ppermute | solution.py:16
  96.4 1.6 collective-permute-done.7.y30.refs_8_
  98.0 3.2 %shard_map.106 = (bf16[384,384]{1,0:T(8,128)(2,1)S(1)}, bf16[384,384]{1,0:T(8,128)(2,1)S(1)}, bf16[384,384]{1,0:T(8,128)(2,1)S(1)}, bf16[384,512]{1,0:T(8,128)(2,1)S(1)}, bf16[384,768]{1,0:T(8,128)(2,1)S(1)}) custom-call(s32[1]{0:T(128)} %bitcast.1.refs_0_.me_ref, bf16[384,640]{1,0:T(8,128)(2,1)S(1)} %collective-permute-done.5.x30.refs_3_, ...), custom_call_target="tpu_custom_call" | custom-call | flops 3774873600 | tf_op jit(solution)/shard_map/pallas_call | solution.py:208
  101.2 0.3 collective-permute-start.9
  101.5 2.7 %collective-permute-start.11 = (bf16[384,768]{1,0:T(8,128)(2,1)S(1)}, bf16[384,768]{1,0:T(8,128)(2,1)S(1)}, u32[]{:S(2)}, u32[]{:S(2)}) collective-permute-start(bf16[384,768]{1,0:T(8,128)(2,1)S(1)} %get-tuple-element.67), channel_id=1, source_target_pairs={{0,3},{1,0},{2,1},{3,2},{4,7},{5,4},{6,5},{7,6},{8,11},{9,8},{10,9... | collective-permute-start | bytes 1769480 | tf_op jit(solution)/shard_map/ppermute | solution.py:16
  104.1 3.2 %shard_map.107 = (bf16[384,512]{1,0:T(8,128)(2,1)S(1)}, bf16[384,768]{1,0:T(8,128)(2,1)S(1)}, bf16[384,512]{1,0:T(8,128)(2,1)S(1)}, bf16[384,768]{1,0:T(8,128)(2,1)S(1)}, bf16[384,1280]{1,0:T(8,128)(2,1)S(1)}) custom-call(s32[1]{0:T(128)} %bitcast.1.refs_0_.me_ref, bf16[384,384]{1,0:T(8,128)(2,1)S(1)} %get-tuple-element.72.dg_ref.refs_10_, ...), custom_call_target="tpu_custom_call" | custom-call | flops 4529848320 | tf_op jit(solution)/shard_map/pallas_call | solution.py:208
  107.4 0.1 collective-permute-start.14
  107.5 2.8 %collective-permute-done.9 = bf16[384,512]{1,0:T(8,128)(2,1)S(1)} collective-permute-done((bf16[384,512]{1,0:T(8,128)(2,1)S(1)}, bf16[384,512]{1,0:T(8,128)(2,1)S(1)}, u32[]{:S(2)}, u32[]{:S(2)}) %collective-permute-start.9) | collective-permute-done | bytes 393248 | tf_op jit(solution)/shard_map/ppermute | solution.py:16
  110.3 0.1 add_convert_fusion.1
  110.4 0.1 collective-permute-start.13
  110.5 0.1 collective-permute-start.10
  110.6 2.9 %collective-permute-done.11 = bf16[384,768]{1,0:T(8,128)(2,1)S(1)} collective-permute-done((bf16[384,768]{1,0:T(8,128)(2,1)S(1)}, bf16[384,768]{1,0:T(8,128)(2,1)S(1)}, u32[]{:S(2)}, u32[]{:S(2)}) %collective-permute-start.11) | collective-permute-done | bytes 589856 | tf_op jit(solution)/shard_map/ppermute | solution.py:16
  113.5 0.2 add_convert_fusion
  113.7 3.5 %collective-permute-start.12 = (bf16[384,768]{1,0:T(8,128)(2,1)S(1)}, bf16[384,768]{1,0:T(8,128)(2,1)S(1)}, u32[]{:S(2)}, u32[]{:S(2)}) collective-permute-start(bf16[384,768]{1,0:T(8,128)(2,1)S(1)} %add_convert_fusion), channel_id=1, source_target_pairs={{0,3},{1,0},{2,1},{3,2},{4,7},{5,4},{6,5},{7,6},{8,11},{9,8},{10,9... | collective-permute-start | bytes 1769480 | tf_op jit(solution)/shard_map/ppermute | solution.py:16
  117.1 4.8 %collective-permute-done.14.r_ref = bf16[384,512]{1,0:T(8,128)(2,1)S(1)} collective-permute-done((bf16[384,512]{1,0:T(8,128)(2,1)S(1)}, bf16[384,512]{1,0:T(8,128)(2,1)S(1)}, u32[]{:S(2)}, u32[]{:S(2)}) %collective-permute-start.14) | collective-permute-done | bytes 393248 | tf_op jit(solution)/shard_map/ppermute | solution.py:16
  121.9 0.2 shard_map.108
  122.1 2.7 %collective-permute-start.15 = (bf16[384,512]{1,0:T(8,128)(2,1)S(1)}, bf16[384,512]{1,0:T(8,128)(2,1)S(1)}, u32[]{:S(2)}, u32[]{:S(2)}) collective-permute-start(bf16[384,512]{1,0:T(8,128)(2,1)S(1)} %shard_map.108), channel_id=1, source_target_pairs={{0,64},{64,0},{1,65},{65,1},{2,66},{66,2},{3,67},{67,3},{4,68},{68... | collective-permute-start | bytes 1179656 | tf_op jit(solution)/shard_map/ppermute | solution.py:16
  124.8 6.3 %collective-permute-done.10.l_ref = bf16[384,768]{1,0:T(8,128)(2,1)S(1)} collective-permute-done((bf16[384,768]{1,0:T(8,128)(2,1)S(1)}, bf16[384,768]{1,0:T(8,128)(2,1)S(1)}, u32[]{:S(2)}, u32[]{:S(2)}) %collective-permute-start.10) | collective-permute-done | bytes 589856 | tf_op jit(solution)/shard_map/ppermute | solution.py:16
  131.0 3.5 %collective-permute-done.12.r_ref = bf16[384,768]{1,0:T(8,128)(2,1)S(1)} collective-permute-done((bf16[384,768]{1,0:T(8,128)(2,1)S(1)}, bf16[384,768]{1,0:T(8,128)(2,1)S(1)}, u32[]{:S(2)}, u32[]{:S(2)}) %collective-permute-start.12) | collective-permute-done | bytes 589856 | tf_op jit(solution)/shard_map/ppermute | solution.py:16
  134.6 1.3 shard_map.109
  135.9 11.5 %all-to-all-start.2 = ((bf16[32,24,768]{2,1,0:T(8,128)(2,1)}), bf16[32,24,768]{2,1,0:T(8,128)(2,1)S(1)}, u32[]{:S(2)}, u32[]{:S(2)}) async-start(bf16[32,24,768]{2,1,0:T(8,128)(2,1)} %bitcast.14), calls=%async_computation.2 | async-start | bytes 2359296 | tf_op jit(solution)/shard_map/all_to_all | solution.py:347
  147.4 13.2 %shard_map.111 = (bf16[5120,384]{1,0:T(8,128)(2,1)}, bf16[5120,384]{1,0:T(8,128)(2,1)}, bf16[384,5120]{1,0:T(8,128)(2,1)}) custom-call(s32[1]{0:T(128)} %bitcast.1.refs_0_.me_ref, bf16[384,1280]{1,0:T(8,128)(2,1)} %bitcast.37, bf16[384,1280]{1,0:T(8,128)(2,1)} %copy-done.11, bf16[384,1280]{1,0:T(8,128)(2,1)} %copy-done.10, bf16[384,640]{1,0:T(8,128)(2,1)} %copy-done.7, ...), custom_call_target="tpu_custom_call" | custom-call | flops 9059696640 | tf_op jit(solution)/shard_map/pallas_call | solution.py:329
  160.6 5.2 %all-to-all-done.2 = bf16[32,24,768]{2,1,0:T(8,128)(2,1)S(1)} async-done(((bf16[32,24,768]{2,1,0:T(8,128)(2,1)}), bf16[32,24,768]{2,1,0:T(8,128)(2,1)S(1)}, u32[]{:S(2)}, u32[]{:S(2)}) %all-to-all-start.2) | async-done | bytes 1179680 | tf_op jit(solution)/shard_map/all_to_all | solution.py:347
  165.7 1.7 shard_map.110
  (46 shorter events, 0.3 us)
Async XLA Ops:
  1.3 1.2 copy-start.14
  2.5 0.7 copy-start.19
  3.2 10.0 %copy-start.15 = (bf16[1,384,1280]{2,1,0:T(8,128)(2,1)S(1)}, bf16[1,384,1280]{2,1,0:T(8,128)(2,1)}, u32[]{:S(2)}) copy-start(bf16[1,384,1280]{2,1,0:T(8,128)(2,1)} %param.8) | copy-start | bytes 2949124
  5.4 22.9 %all-to-all-start = ((bf16[16,24,1280]{2,1,0:T(8,128)(2,1)}), bf16[16,24,1280]{2,1,0:T(8,128)(2,1)S(1)}, u32[]{:S(2)}, u32[]{:S(2)}) async-start(bf16[16,24,1280]{2,1,0:T(8,128)(2,1)} %bitcast.7), calls=%async_computation | async-start | bytes 1966080 | tf_op jit(solution)/shard_map/all_to_all | solution.py:256
  28.3 37.2 %copy-start.4 = (bf16[16,24,1280]{2,1,0:T(8,128)(2,1)}, bf16[16,24,1280]{2,1,0:T(8,128)(2,1)S(1)}, u32[]{:S(2)}) copy-start(bf16[16,24,1280]{2,1,0:T(8,128)(2,1)S(1)} %all-to-all-done) | copy-start | bytes 2949124
  28.3 31.6 %copy-start.1 = (bf16[1,1,5120,384]{3,2,1,0:T(8,128)(2,1)S(1)}, bf16[1,1,5120,384]{3,2,1,0:T(8,128)(2,1)}, u32[]{:S(2)}) copy-start(bf16[1,1,5120,384]{3,2,1,0:T(8,128)(2,1)} %param.11) | copy-start | bytes 11796484
  28.3 22.7 %collective-permute-start.1 = (bf16[384,1280]{1,0:T(8,128)(2,1)S(1)}, bf16[384,1280]{1,0:T(8,128)(2,1)S(1)}, u32[]{:S(2)}, u32[]{:S(2)}) collective-permute-start(bf16[384,1280]{1,0:T(8,128)(2,1)S(1)} %bitcast.34), channel_id=1, source_target_pairs={{0,3},{1,0},{2,1},{3,2},{4,7},{5,4},{6,5},{7,6},{8,11},{9,8},{10,9... | collective-permute-start | bytes 2949128 | tf_op jit(solution)/shard_map/ppermute | solution.py:16
  30.8 23.3 %collective-permute-start = (bf16[384,1280]{1,0:T(8,128)(2,1)S(1)}, bf16[384,1280]{1,0:T(8,128)(2,1)S(1)}, u32[]{:S(2)}, u32[]{:S(2)}) collective-permute-start(bf16[384,1280]{1,0:T(8,128)(2,1)S(1)} %bitcast.35), channel_id=1, source_target_pairs={{0,1},{1,2},{2,3},{3,0},{4,5},{5,6},{6,7},{7,4},{8,9},{9,10},{10,1... | collective-permute-start | bytes 2949128 | tf_op jit(solution)/shard_map/ppermute | solution.py:16
  49.2 29.3 %copy-start.5 = (bf16[16,24,1280]{2,1,0:T(8,128)(2,1)}, bf16[16,24,1280]{2,1,0:T(8,128)(2,1)S(1)}, u32[]{:S(2)}) copy-start(bf16[16,24,1280]{2,1,0:T(8,128)(2,1)S(1)} %all_to_all.15) | copy-start | bytes 2949124
  51.0 14.6 %copy-start.10 = (bf16[384,1280]{1,0:T(8,128)(2,1)}, bf16[384,1280]{1,0:T(8,128)(2,1)S(1)}, u32[]{:S(2)}) copy-start(bf16[384,1280]{1,0:T(8,128)(2,1)S(1)} %collective-permute-done.1.refs_4_.refs_2_) | copy-start | bytes 2949124
  54.1 11.5 %copy-start.11 = (bf16[384,1280]{1,0:T(8,128)(2,1)}, bf16[384,1280]{1,0:T(8,128)(2,1)S(1)}, u32[]{:S(2)}) copy-start(bf16[384,1280]{1,0:T(8,128)(2,1)S(1)} %collective-permute-done.refs_3_.refs_1_) | copy-start | bytes 2949124
  54.1 21.2 %collective-permute-start.3 = (bf16[384,1280]{1,0:T(8,128)(2,1)S(1)}, bf16[384,1280]{1,0:T(8,128)(2,1)S(1)}, u32[]{:S(2)}, u32[]{:S(2)}) collective-permute-start(bf16[384,1280]{1,0:T(8,128)(2,1)S(1)} %bitcast.38), channel_id=1, source_target_pairs={{0,3},{1,0},{2,1},{3,2},{4,7},{5,4},{6,5},{7,6},{8,11},{9,8},{10,9... | collective-permute-start | bytes 2949128 | tf_op jit(solution)/shard_map/ppermute | solution.py:16
  54.5 22.4 %collective-permute-start.2 = (bf16[384,1280]{1,0:T(8,128)(2,1)S(1)}, bf16[384,1280]{1,0:T(8,128)(2,1)S(1)}, u32[]{:S(2)}, u32[]{:S(2)}) collective-permute-start(bf16[384,1280]{1,0:T(8,128)(2,1)S(1)} %bitcast.39), channel_id=1, source_target_pairs={{0,1},{1,2},{2,3},{3,0},{4,5},{5,6},{6,7},{7,4},{8,9},{9,10},{10,1... | collective-permute-start | bytes 2949128 | tf_op jit(solution)/shard_map/ppermute | solution.py:16
  55.6 4.4 %collective-permute-start.4 = (s32[6,384]{1,0:T(8,128)S(1)}, s32[6,384]{1,0:T(8,128)S(1)}, u32[]{:S(2)}, u32[]{:S(2)}) collective-permute-start(s32[6,384]{1,0:T(8,128)S(1)} %bitcast.44), channel_id=1, source_target_pairs={{0,64},{64,0},{1,65},{65,1},{2,66},{66,2},{3,67},{67,3},{4,68},{68... | collective-permute-start | bytes 27656 | tf_op jit(solution)/shard_map/ppermute | solution.py:16
  58.3 27.5 %collective-permute-start.6 = (bf16[384,640]{1,0:T(8,128)(2,1)S(1)}, bf16[384,640]{1,0:T(8,128)(2,1)S(1)}, u32[]{:S(2)}, u32[]{:S(2)}) collective-permute-start(bf16[384,640]{1,0:T(8,128)(2,1)S(1)} %slice.13), channel_id=1, source_target_pairs={{0,3},{1,0},{2,1},{3,2},{4,7},{5,4},{6,5},{7,6},{8,11},{9,8},{10,9... | collective-permute-start | bytes 1474568 | tf_op jit(solution)/shard_map/ppermute | solution.py:16
  60.0 27.5 %collective-permute-start.5 = (bf16[384,640]{1,0:T(8,128)(2,1)S(1)}, bf16[384,640]{1,0:T(8,128)(2,1)S(1)}, u32[]{:S(2)}, u32[]{:S(2)}) collective-permute-start(bf16[384,640]{1,0:T(8,128)(2,1)S(1)} %slice.12), channel_id=1, source_target_pairs={{0,1},{1,2},{2,3},{3,0},{4,5},{5,6},{6,7},{7,4},{8,9},{9,10},{10,1... | collective-permute-start | bytes 1474568 | tf_op jit(solution)/shard_map/ppermute | solution.py:16
  60.0 2.1 %copy-start.2 = (bf16[1,1,5120,384]{3,2,1,0:T(8,128)(2,1)S(1)}, bf16[1,1,5120,384]{3,2,1,0:T(8,128)(2,1)}, u32[]{:S(2)}) copy-start(bf16[1,1,5120,384]{3,2,1,0:T(8,128)(2,1)} %param.12) | copy-start | bytes 11796484
  62.1 16.5 %copy-start = (bf16[1,1,384,5120]{3,2,1,0:T(8,128)(2,1)S(1)}, bf16[1,1,384,5120]{3,2,1,0:T(8,128)(2,1)}, u32[]{:S(2)}) copy-start(bf16[1,1,384,5120]{3,2,1,0:T(8,128)(2,1)} %param.13) | copy-start | bytes 11796484
  75.3 5.0 %copy-start.12 = (bf16[384,1280]{1,0:T(8,128)(2,1)}, bf16[384,1280]{1,0:T(8,128)(2,1)S(1)}, u32[]{:S(2)}) copy-start(bf16[384,1280]{1,0:T(8,128)(2,1)S(1)} %collective-permute-done.3.y2.refs_7_) | copy-start | bytes 2949124
  76.9 3.4 %copy-start.13 = (bf16[384,1280]{1,0:T(8,128)(2,1)}, bf16[384,1280]{1,0:T(8,128)(2,1)S(1)}, u32[]{:S(2)}) copy-start(bf16[384,1280]{1,0:T(8,128)(2,1)S(1)} %collective-permute-done.2.y1.refs_6_) | copy-start | bytes 2949124
  77.0 19.4 %collective-permute-start.8 = (bf16[384,640]{1,0:T(8,128)(2,1)S(1)}, bf16[384,640]{1,0:T(8,128)(2,1)S(1)}, u32[]{:S(2)}, u32[]{:S(2)}) collective-permute-start(bf16[384,640]{1,0:T(8,128)(2,1)S(1)} %slice.15), channel_id=1, source_target_pairs={{0,3},{1,0},{2,1},{3,2},{4,7},{5,4},{6,5},{7,6},{8,11},{9,8},{10,9... | collective-permute-start | bytes 1474568 | tf_op jit(solution)/shard_map/ppermute | solution.py:16
  77.4 20.6 %collective-permute-start.7 = (bf16[384,640]{1,0:T(8,128)(2,1)S(1)}, bf16[384,640]{1,0:T(8,128)(2,1)S(1)}, u32[]{:S(2)}, u32[]{:S(2)}) collective-permute-start(bf16[384,640]{1,0:T(8,128)(2,1)S(1)} %slice.14), channel_id=1, source_target_pairs={{0,1},{1,2},{2,3},{3,0},{4,5},{5,6},{6,7},{7,4},{8,9},{9,10},{10,1... | collective-permute-start | bytes 1474568 | tf_op jit(solution)/shard_map/ppermute | solution.py:16
  78.5 19.4 %copy-start.3 = (bf16[1,1,5120,384]{3,2,1,0:T(8,128)(2,1)S(1)}, bf16[1,1,5120,384]{3,2,1,0:T(8,128)(2,1)}, u32[]{:S(2)}) copy-start(bf16[1,1,5120,384]{3,2,1,0:T(8,128)(2,1)} %param.12) | copy-start | bytes 11796484
  85.8 15.3 %copy-start.6 = (bf16[384,640]{1,0:T(8,128)(2,1)}, bf16[384,640]{1,0:T(8,128)(2,1)S(1)}, u32[]{:S(2)}) copy-start(bf16[384,640]{1,0:T(8,128)(2,1)S(1)} %collective-permute-done.6.x31.refs_4_) | copy-start | bytes 1474564
  87.4 13.7 %copy-start.7 = (bf16[384,640]{1,0:T(8,128)(2,1)}, bf16[384,640]{1,0:T(8,128)(2,1)S(1)}, u32[]{:S(2)}) copy-start(bf16[384,640]{1,0:T(8,128)(2,1)S(1)} %collective-permute-done.5.x30.refs_3_) | copy-start | bytes 1474564
  96.4 4.8 %copy-start.8 = (bf16[384,640]{1,0:T(8,128)(2,1)}, bf16[384,640]{1,0:T(8,128)(2,1)S(1)}, u32[]{:S(2)}) copy-start(bf16[384,640]{1,0:T(8,128)(2,1)S(1)} %collective-permute-done.8.y31.refs_9_) | copy-start | bytes 1474564
  98.0 3.2 %copy-start.9 = (bf16[384,640]{1,0:T(8,128)(2,1)}, bf16[384,640]{1,0:T(8,128)(2,1)S(1)}, u32[]{:S(2)}) copy-start(bf16[384,640]{1,0:T(8,128)(2,1)S(1)} %collective-permute-done.7.y30.refs_8_) | copy-start | bytes 1474564
  101.2 6.2 %copy-start.16 = (bf16[384,384]{1,0:T(8,128)(2,1)}, bf16[384,384]{1,0:T(8,128)(2,1)S(1)}, u32[]{:S(2)}) copy-start(bf16[384,384]{1,0:T(8,128)(2,1)S(1)} %get-tuple-element.72.dg_ref.refs_10_) | copy-start | bytes 884740
  101.2 6.2 %copy-start.17 = (bf16[384,384]{1,0:T(8,128)(2,1)}, bf16[384,384]{1,0:T(8,128)(2,1)S(1)}, u32[]{:S(2)}) copy-start(bf16[384,384]{1,0:T(8,128)(2,1)S(1)} %get-tuple-element.73.du_ref.refs_11_) | copy-start | bytes 884740
  101.2 6.2 %copy-start.18 = (bf16[384,384]{1,0:T(8,128)(2,1)}, bf16[384,384]{1,0:T(8,128)(2,1)S(1)}, u32[]{:S(2)}) copy-start(bf16[384,384]{1,0:T(8,128)(2,1)S(1)} %get-tuple-element.74.refs_12_) | copy-start | bytes 884740
  101.2 9.1 %collective-permute-start.9 = (bf16[384,512]{1,0:T(8,128)(2,1)S(1)}, bf16[384,512]{1,0:T(8,128)(2,1)S(1)}, u32[]{:S(2)}, u32[]{:S(2)}) collective-permute-start(bf16[384,512]{1,0:T(8,128)(2,1)S(1)} %get-tuple-element.63), channel_id=1, source_target_pairs={{0,1},{1,2},{2,3},{3,0},{4,5},{5,6},{6,7},{7,4},{8,9},{9,10},{10,1... | collective-permute-start | bytes 1179656 | tf_op jit(solution)/shard_map/ppermute | solution.py:16
  101.5 12.0 %collective-permute-start.11 = (bf16[384,768]{1,0:T(8,128)(2,1)S(1)}, bf16[384,768]{1,0:T(8,128)(2,1)S(1)}, u32[]{:S(2)}, u32[]{:S(2)}) collective-permute-start(bf16[384,768]{1,0:T(8,128)(2,1)S(1)} %get-tuple-element.67), channel_id=1, source_target_pairs={{0,3},{1,0},{2,1},{3,2},{4,7},{5,4},{6,5},{7,6},{8,11},{9,8},{10,9... | collective-permute-start | bytes 1769480 | tf_op jit(solution)/shard_map/ppermute | solution.py:16
  107.4 14.5 %collective-permute-start.14 = (bf16[384,512]{1,0:T(8,128)(2,1)S(1)}, bf16[384,512]{1,0:T(8,128)(2,1)S(1)}, u32[]{:S(2)}, u32[]{:S(2)}) collective-permute-start(bf16[384,512]{1,0:T(8,128)(2,1)S(1)} %get-tuple-element.69), channel_id=1, source_target_pairs={{0,3},{1,0},{2,1},{3,2},{4,7},{5,4},{6,5},{7,6},{8,11},{9,8},{10,9... | collective-permute-start | bytes 1179656 | tf_op jit(solution)/shard_map/ppermute | solution.py:16
  110.4 11.5 %collective-permute-start.13 = (bf16[384,512]{1,0:T(8,128)(2,1)S(1)}, bf16[384,512]{1,0:T(8,128)(2,1)S(1)}, u32[]{:S(2)}, u32[]{:S(2)}) collective-permute-start(bf16[384,512]{1,0:T(8,128)(2,1)S(1)} %add_convert_fusion.1), channel_id=1, source_target_pairs={{0,1},{1,2},{2,3},{3,0},{4,5},{5,6},{6,7},{7,4},{8,9},{9,10},{10,1... | collective-permute-start | bytes 1179656 | tf_op jit(solution)/shard_map/ppermute | solution.py:16
  110.5 20.6 %collective-permute-start.10 = (bf16[384,768]{1,0:T(8,128)(2,1)S(1)}, bf16[384,768]{1,0:T(8,128)(2,1)S(1)}, u32[]{:S(2)}, u32[]{:S(2)}) collective-permute-start(bf16[384,768]{1,0:T(8,128)(2,1)S(1)} %get-tuple-element.65), channel_id=1, source_target_pairs={{0,1},{1,2},{2,3},{3,0},{4,5},{5,6},{6,7},{7,4},{8,9},{9,10},{10,1... | collective-permute-start | bytes 1769480 | tf_op jit(solution)/shard_map/ppermute | solution.py:16
  113.7 20.9 %collective-permute-start.12 = (bf16[384,768]{1,0:T(8,128)(2,1)S(1)}, bf16[384,768]{1,0:T(8,128)(2,1)S(1)}, u32[]{:S(2)}, u32[]{:S(2)}) collective-permute-start(bf16[384,768]{1,0:T(8,128)(2,1)S(1)} %add_convert_fusion), channel_id=1, source_target_pairs={{0,3},{1,0},{2,1},{3,2},{4,7},{5,4},{6,5},{7,6},{8,11},{9,8},{10,9... | collective-permute-start | bytes 1769480 | tf_op jit(solution)/shard_map/ppermute | solution.py:16
  122.1 12.5 %collective-permute-start.15 = (bf16[384,512]{1,0:T(8,128)(2,1)S(1)}, bf16[384,512]{1,0:T(8,128)(2,1)S(1)}, u32[]{:S(2)}, u32[]{:S(2)}) collective-permute-start(bf16[384,512]{1,0:T(8,128)(2,1)S(1)} %shard_map.108), channel_id=1, source_target_pairs={{0,64},{64,0},{1,65},{65,1},{2,66},{66,2},{3,67},{67,3},{4,68},{68... | collective-permute-start | bytes 1179656 | tf_op jit(solution)/shard_map/ppermute | solution.py:16
  135.9 29.9 %all-to-all-start.2 = ((bf16[32,24,768]{2,1,0:T(8,128)(2,1)}), bf16[32,24,768]{2,1,0:T(8,128)(2,1)S(1)}, u32[]{:S(2)}, u32[]{:S(2)}) async-start(bf16[32,24,768]{2,1,0:T(8,128)(2,1)} %bitcast.14), calls=%async_computation.2 | async-start | bytes 2359296 | tf_op jit(solution)/shard_map/all_to_all | solution.py:347

commit v4 on v3

--- a/solution.py
+++ b/solution.py
@@ -215,7 +215,7 @@
     )(*scalars, *arrays)
 
 
-SHIFTED = 512
+SHIFTED = 640
 ORDER = (0, 3, 1, 2)
 
 
@@ -307,12 +307,12 @@
     def added(a, b):
         return (a.astype(jnp.float32) + b.astype(jnp.float32)).astype(jnp.bfloat16)
 
-    right0, right1 = lax.optimization_barrier((added(right0, far0), right1))
-    from_left0 = passed_along(right0, "edp", 1)
     from_right0 = passed_along(left0, "edp", -1)
+    from_left0 = passed_along(added(right0, far0), "edp", 1)
+    (shifted,) = call(sum_kernel, parts[:1], (), (own, from_left0, from_right0))
+    shifted, right1, left1 = lax.optimization_barrier((shifted, right1, added(left1, far1)))
     from_left1 = passed_along(right1, "edp", 1)
-    from_right1 = passed_along(added(left1, far1), "edp", -1)
-    (shifted,) = call(sum_kernel, parts[:1], (), (own, from_left0, from_right0))
+    from_right1 = passed_along(left1, "edp", -1)
     shifted = passed_along(shifted, "section", -1)
     (packed,) = call(
         pack_kernel,

time: 168 us -> 170 us (1.012)
  starting transfers between devices: 38.4 us -> 40.6 us
    all_to_all x1, starting transfers between devices: 11.5 us -> 14.7 us  [body(): lax.all_to_all(packed.reshape(2 * ep_count, CAP, -1), ('section', 'ep'),...]
    all_to_all x1, waiting for transfers between devices: 5.18 us -> 3.01 us  [body(): lax.all_to_all(packed.reshape(2 * ep_count, CAP, -1), ('section', 'ep'),...]
    unnamed x41 -> x45, local copies, waits for them, and re-layouts: 4.77 us -> 5.46 us
where the time goes in v4:
time: 170 us; the launch traced here: 169 us
  waiting for transfers between devices  72.7 us (43%)
  starting transfers between devices  40.6 us (24%)
  Pallas kernels  30.9 us (18%)
  blocking collectives  18.4 us (11%)
  local copies, waits for them, and re-layouts  5.63 us (3%)
    ppermute x16, waiting for transfers between devices, passed_along(): lax.ppermute(array, axis, [(i, (i + by) % length) for i in range(length)])  55.3 us
    all_to_all x1, blocking collectives, to_experts(): lax.all_to_all(shaped, 'ep', split_axis=0, concat_axis=0, tiled=True)  18.4 us
    ppermute x16, starting transfers between devices, passed_along(): lax.ppermute(array, axis, [(i, (i + by) % length) for i in range(length)])  18.1 us
    pallas_call x9, Pallas kernels, call(): pl.pallas_call(kernel, out_shape=outs, in_specs=[IN_SMEM] * len(scalars)...  17.7 us
    all_to_all x1, starting transfers between devices, body(): lax.all_to_all(packed.reshape(2 * ep_count, CAP, -1), ('section', 'ep'),...  14.7 us
    all_to_all x1, waiting for transfers between devices, to_experts(): lax.all_to_all(shaped, 'ep', split_axis=0, concat_axis=0, tiled=True)  14.4 us
    pallas_call x1, Pallas kernels, body(): pl.pallas_call(grad_kernel, out_shape=[bf16(4 * width, hidden)] * 2 + [bf...  13.2 us
    all_to_all x1, starting transfers between devices, to_experts(): lax.all_to_all(shaped, 'ep', split_axis=0, concat_axis=0, tiled=True)  7.84 us
  transfers between devices with their start and end apart: 18, of which 15 were waited for; matrix products, arithmetic and copies ran while one was open for 0% of the time, Pallas kernels for 13%

profile of v4, /device:TPU:1, one launch (start us, length us, event | category | flops | bytes accessed | tf_op | source)
XLA Modules:
  0.0 169.3 jit_solution(8951780172744993753)
XLA Ops:
  0.6 0.7 copy.13
  1.3 1.2 copy-done.14
  2.5 0.7 copy-done.19
  3.2 2.2 %shard_map.102 = (bf16[384,1280]{1,0:T(8,128)(2,1)}, bf16[384,384]{1,0:T(8,128)(2,1)S(1)}) custom-call(s32[6,384]{1,0:T(8,128)S(1)} %bitcast.43, bf16[6,384]{1,0:T(8,128)(2,1)S(1)} %bitcast.47, bf16[384,1280]{1,0:T(8,128)(2,1)S(1)} %bitcast.45), custom_call_target="tpu_custom_call" | custom-call | flops 981467136 | tf_op jit(solution)/shard_map/pallas_call | solution.py:208
  5.4 7.8 %all-to-all-start = ((bf16[16,24,1280]{2,1,0:T(8,128)(2,1)}), bf16[16,24,1280]{2,1,0:T(8,128)(2,1)S(1)}, u32[]{:S(2)}, u32[]{:S(2)}) async-start(bf16[16,24,1280]{2,1,0:T(8,128)(2,1)} %bitcast.7), calls=%async_computation | async-start | bytes 1966080 | tf_op jit(solution)/shard_map/all_to_all | solution.py:256
  13.2 0.7 shard_map.103
  13.9 14.4 %all-to-all-done = bf16[16,24,1280]{2,1,0:T(8,128)(2,1)S(1)} async-done(((bf16[16,24,1280]{2,1,0:T(8,128)(2,1)}), bf16[16,24,1280]{2,1,0:T(8,128)(2,1)S(1)}, u32[]{:S(2)}, u32[]{:S(2)}) %all-to-all-start) | async-done | bytes 983072 | tf_op jit(solution)/shard_map/all_to_all | solution.py:256
  28.3 2.5 %collective-permute-start.1 = (bf16[384,1280]{1,0:T(8,128)(2,1)S(1)}, bf16[384,1280]{1,0:T(8,128)(2,1)S(1)}, u32[]{:S(2)}, u32[]{:S(2)}) collective-permute-start(bf16[384,1280]{1,0:T(8,128)(2,1)S(1)} %bitcast.33), channel_id=1, source_target_pairs={{0,3},{1,0},{2,1},{3,2},{4,7},{5,4},{6,5},{7,6},{8,11},{9,8},{10,9... | collective-permute-start | bytes 2949128 | tf_op jit(solution)/shard_map/ppermute | solution.py:16
  30.8 18.4 %all_to_all.15 = bf16[16,24,1280]{2,1,0:T(8,128)(2,1)S(1)} all-to-all(bf16[16,24,1280]{2,1,0:T(8,128)(2,1)S(1)} %bitcast.42), channel_id=1, replica_groups=mesh['section'=2,'ep'=16,'edp'=4] {'ep'}, dimensions={0} | all-to-all | bytes 1966080 | tf_op jit(solution)/shard_map/all_to_all | solution.py:256
  49.2 1.8 %collective-permute-done.1.refs_4_.refs_2_ = bf16[384,1280]{1,0:T(8,128)(2,1)S(1)} collective-permute-done((bf16[384,1280]{1,0:T(8,128)(2,1)S(1)}, bf16[384,1280]{1,0:T(8,128)(2,1)S(1)}, u32[]{:S(2)}, u32[]{:S(2)}) %collective-permute-start.1) | collective-permute-done | bytes 983072 | tf_op jit(solution)/shard_map/ppermute | solution.py:16
  51.0 3.1 %collective-permute-done.refs_3_.refs_1_ = bf16[384,1280]{1,0:T(8,128)(2,1)S(1)} collective-permute-done((bf16[384,1280]{1,0:T(8,128)(2,1)S(1)}, bf16[384,1280]{1,0:T(8,128)(2,1)S(1)}, u32[]{:S(2)}, u32[]{:S(2)}) %collective-permute-start) | collective-permute-done | bytes 983072 | tf_op jit(solution)/shard_map/ppermute | solution.py:16
  54.1 0.4 collective-permute-start.3
  54.5 1.1 collective-permute-start.2
  55.6 2.6 %collective-permute-start.4 = (s32[6,384]{1,0:T(8,128)S(1)}, s32[6,384]{1,0:T(8,128)S(1)}, u32[]{:S(2)}, u32[]{:S(2)}) collective-permute-start(s32[6,384]{1,0:T(8,128)S(1)} %bitcast.44), channel_id=1, source_target_pairs={{0,64},{64,0},{1,65},{65,1},{2,66},{66,2},{3,67},{67,3},{4,68},{68... | collective-permute-start | bytes 27656 | tf_op jit(solution)/shard_map/ppermute | solution.py:16
  58.3 1.6 collective-permute-start.6
  60.0 2.1 %copy-done.2 = bf16[1,1,5120,384]{3,2,1,0:T(8,128)(2,1)S(1)} copy-done((bf16[1,1,5120,384]{3,2,1,0:T(8,128)(2,1)S(1)}, bf16[1,1,5120,384]{3,2,1,0:T(8,128)(2,1)}, u32[]{:S(2)}) %copy-start.2) | copy-done | bytes 3932184
  62.1 3.5 %shard_map.104 = (f32[384,384]{1,0:T(8,128)S(1)}, f32[384,384]{1,0:T(8,128)S(1)}, bf16[384,384]{1,0:T(8,128)(2,1)S(1)}) custom-call(s32[1]{0:T(128)} %bitcast.1.refs_0_.me_ref, s32[6,384]{1,0:T(8,128)S(1)} %collective-permute-done.4.refs_1_, bf16[384,1280]{1,0:T(8,128)(2,1)S(1)} %bitcast.35, bf16[384,1280]{1,0:T(8,128)(2,1)S(1)} %collective-permute-done.refs_3_.refs_1_, ...), custom_call_target="tpu_custom_call" | custom-call | flops 4529848320 | tf_op jit(solution)/shard_map/pallas_call | solution.py:208
  65.6 9.7 %collective-permute-done.3.y2.refs_7_ = bf16[384,1280]{1,0:T(8,128)(2,1)S(1)} collective-permute-done((bf16[384,1280]{1,0:T(8,128)(2,1)S(1)}, bf16[384,1280]{1,0:T(8,128)(2,1)S(1)}, u32[]{:S(2)}, u32[]{:S(2)}) %collective-permute-start.3) | collective-permute-done | bytes 983072 | tf_op jit(solution)/shard_map/ppermute | solution.py:16
  75.3 1.6 collective-permute-done.2.y1.refs_6_
  77.0 0.4 collective-permute-start.8
  77.4 1.2 collective-permute-start.7
  78.6 1.7 %shard_map.105.back_ref = f32[384,384]{1,0:T(8,128)S(1)} custom-call(s32[1]{0:T(128)} %bitcast.1.refs_0_.me_ref, bf16[384,1280]{1,0:T(8,128)(2,1)S(1)} %bitcast.39, bf16[384,1280]{1,0:T(8,128)(2,1)S(1)} %collective-permute-done.2.y1.refs_6_, bf16[384,1280]{1,0:T(8,128)(2,1)S(1)} %collective-permute-done.3.y2.refs_7_, bf16[384,5120]{1,0:T(8,128)(2,1)S(1)} %bitcast.25), custom_call_target="tpu_custom_call" | custom-call | flops 2264924160 | tf_op jit(solution)/shard_map/pallas_call | solution.py:208
  80.3 5.5 %collective-permute-done.6.x31.refs_4_ = bf16[384,640]{1,0:T(8,128)(2,1)S(1)} collective-permute-done((bf16[384,640]{1,0:T(8,128)(2,1)S(1)}, bf16[384,640]{1,0:T(8,128)(2,1)S(1)}, u32[]{:S(2)}, u32[]{:S(2)}) %collective-permute-start.6) | collective-permute-done | bytes 491552 | tf_op jit(solution)/shard_map/ppermute | solution.py:16
  85.8 1.6 collective-permute-done.5.x30.refs_3_
  87.4 8.9 %collective-permute-done.8.y31.refs_9_ = bf16[384,640]{1,0:T(8,128)(2,1)S(1)} collective-permute-done((bf16[384,640]{1,0:T(8,128)(2,1)S(1)}, bf16[384,640]{1,0:T(8,128)(2,1)S(1)}, u32[]{:S(2)}, u32[]{:S(2)}) %collective-permute-start.8) | collective-permute-done | bytes 491552 | tf_op jit(solution)/shard_map/ppermute | solution.py:16
  96.4 1.6 collective-permute-done.7.y30.refs_8_
  98.0 3.4 %shard_map.106 = (bf16[384,384]{1,0:T(8,128)(2,1)S(1)}, bf16[384,384]{1,0:T(8,128)(2,1)S(1)}, bf16[384,384]{1,0:T(8,128)(2,1)S(1)}, bf16[384,640]{1,0:T(8,128)(2,1)S(1)}, bf16[384,640]{1,0:T(8,128)(2,1)S(1)}) custom-call(s32[1]{0:T(128)} %bitcast.1.refs_0_.me_ref, bf16[384,640]{1,0:T(8,128)(2,1)S(1)} %collective-permute-done.5.x30.refs_3_, ...), custom_call_target="tpu_custom_call" | custom-call | flops 3774873600 | tf_op jit(solution)/shard_map/pallas_call | solution.py:208
  101.4 0.7 copy-done.18
  102.1 2.7 %collective-permute-start.12 = (bf16[384,640]{1,0:T(8,128)(2,1)S(1)}, bf16[384,640]{1,0:T(8,128)(2,1)S(1)}, u32[]{:S(2)}, u32[]{:S(2)}) collective-permute-start(bf16[384,640]{1,0:T(8,128)(2,1)S(1)} %get-tuple-element.68), channel_id=1, source_target_pairs={{0,3},{1,0},{2,1},{3,2},{4,7},{5,4},{6,5},{7,6},{8,11},{9,8},{10,9... | collective-permute-start | bytes 1474568 | tf_op jit(solution)/shard_map/ppermute | solution.py:16
  104.8 3.2 %shard_map.107 = (bf16[384,640]{1,0:T(8,128)(2,1)S(1)}, bf16[384,640]{1,0:T(8,128)(2,1)S(1)}, bf16[384,640]{1,0:T(8,128)(2,1)S(1)}, bf16[384,640]{1,0:T(8,128)(2,1)S(1)}, bf16[384,1280]{1,0:T(8,128)(2,1)S(1)}) custom-call(s32[1]{0:T(128)} %bitcast.1.refs_0_.me_ref, bf16[384,384]{1,0:T(8,128)(2,1)S(1)} %get-tuple-element.74.dg_ref.refs_10_, ...), custom_call_target="tpu_custom_call" | custom-call | flops 4529848320 | tf_op jit(solution)/shard_map/pallas_call | solution.py:208
  108.0 0.1 collective-permute-start.11
  108.1 4.9 %collective-permute-done.9 = bf16[384,640]{1,0:T(8,128)(2,1)S(1)} collective-permute-done((bf16[384,640]{1,0:T(8,128)(2,1)S(1)}, bf16[384,640]{1,0:T(8,128)(2,1)S(1)}, u32[]{:S(2)}, u32[]{:S(2)}) %collective-permute-start.9) | collective-permute-done | bytes 491552 | tf_op jit(solution)/shard_map/ppermute | solution.py:16
  113.0 0.1 add_convert_fusion.1
  113.2 0.1 collective-permute-start.10
  113.3 0.1 add_convert_fusion
  113.4 9.2 %collective-permute-done.11.r_ref = bf16[384,640]{1,0:T(8,128)(2,1)S(1)} collective-permute-done((bf16[384,640]{1,0:T(8,128)(2,1)S(1)}, bf16[384,640]{1,0:T(8,128)(2,1)S(1)}, u32[]{:S(2)}, u32[]{:S(2)}) %collective-permute-start.11) | collective-permute-done | bytes 491552 | tf_op jit(solution)/shard_map/ppermute | solution.py:16
  122.6 0.7 collective-permute-done.10.l_ref
  123.3 0.2 shard_map.108
  123.5 0.1 collective-permute-start.13
  123.5 2.8 %collective-permute-start.14 = (bf16[384,640]{1,0:T(8,128)(2,1)S(1)}, bf16[384,640]{1,0:T(8,128)(2,1)S(1)}, u32[]{:S(2)}, u32[]{:S(2)}) collective-permute-start(bf16[384,640]{1,0:T(8,128)(2,1)S(1)} %add_convert_fusion), channel_id=1, source_target_pairs={{0,3},{1,0},{2,1},{3,2},{4,7},{5,4},{6,5},{7,6},{8,11},{9,8},{10,9... | collective-permute-start | bytes 1474568 | tf_op jit(solution)/shard_map/ppermute | solution.py:16
  126.3 2.6 %collective-permute-start.15 = (bf16[384,640]{1,0:T(8,128)(2,1)S(1)}, bf16[384,640]{1,0:T(8,128)(2,1)S(1)}, u32[]{:S(2)}, u32[]{:S(2)}) collective-permute-start(bf16[384,640]{1,0:T(8,128)(2,1)S(1)} %shard_map.108), channel_id=1, source_target_pairs={{0,64},{64,0},{1,65},{65,1},{2,66},{66,2},{3,67},{67,3},{4,68},{68... | collective-permute-start | bytes 1474568 | tf_op jit(solution)/shard_map/ppermute | solution.py:16
  128.9 4.0 %collective-permute-done.13.l_ref = bf16[384,640]{1,0:T(8,128)(2,1)S(1)} collective-permute-done((bf16[384,640]{1,0:T(8,128)(2,1)S(1)}, bf16[384,640]{1,0:T(8,128)(2,1)S(1)}, u32[]{:S(2)}, u32[]{:S(2)}) %collective-permute-start.13) | collective-permute-done | bytes 491552 | tf_op jit(solution)/shard_map/ppermute | solution.py:16
  133.0 2.5 %collective-permute-done.15.shifted_ref = bf16[384,640]{1,0:T(8,128)(2,1)S(1)} collective-permute-done((bf16[384,640]{1,0:T(8,128)(2,1)S(1)}, bf16[384,640]{1,0:T(8,128)(2,1)S(1)}, u32[]{:S(2)}, u32[]{:S(2)}) %collective-permute-start.15) | collective-permute-done | bytes 491552 | tf_op jit(solution)/shard_map/ppermute | solution.py:16
  135.5 1.2 shard_map.109
  136.7 14.7 %all-to-all-start.2 = ((bf16[32,24,640]{2,1,0:T(8,128)(2,1)}), bf16[32,24,640]{2,1,0:T(8,128)(2,1)S(1)}, u32[]{:S(2)}, u32[]{:S(2)}) async-start(bf16[32,24,640]{2,1,0:T(8,128)(2,1)} %bitcast.14), calls=%async_computation.2 | async-start | bytes 1966080 | tf_op jit(solution)/shard_map/all_to_all | solution.py:347
  151.4 13.2 %shard_map.111 = (bf16[5120,384]{1,0:T(8,128)(2,1)}, bf16[5120,384]{1,0:T(8,128)(2,1)}, bf16[384,5120]{1,0:T(8,128)(2,1)}) custom-call(s32[1]{0:T(128)} %bitcast.1.refs_0_.me_ref, bf16[384,1280]{1,0:T(8,128)(2,1)} %bitcast.36, bf16[384,1280]{1,0:T(8,128)(2,1)} %copy-done.11, bf16[384,1280]{1,0:T(8,128)(2,1)} %copy-done.10, bf16[384,640]{1,0:T(8,128)(2,1)} %copy-done.7, ...), custom_call_target="tpu_custom_call" | custom-call | flops 9059696640 | tf_op jit(solution)/shard_map/pallas_call | solution.py:329
  164.5 3.0 %all-to-all-done.2 = bf16[32,24,640]{2,1,0:T(8,128)(2,1)S(1)} async-done(((bf16[32,24,640]{2,1,0:T(8,128)(2,1)}), bf16[32,24,640]{2,1,0:T(8,128)(2,1)S(1)}, u32[]{:S(2)}, u32[]{:S(2)}) %all-to-all-start.2) | async-done | bytes 983072 | tf_op jit(solution)/shard_map/all_to_all | solution.py:347
  167.5 1.7 %shard_map.110 = bf16[384,1280]{1,0:T(8,128)(2,1)} custom-call(s32[1]{0:T(128)} %bitcast.2.section_ref, bf16[384,384]{1,0:T(8,128)(2,1)S(1)} %copy-done.21, bf16[768,640]{1,0:T(8,128)(2,1)S(1)} %bitcast.41), custom_call_target="tpu_custom_call" | custom-call | flops 754974720 | tf_op jit(solution)/shard_map/pallas_call | solution.py:208
  (50 shorter events, 0.3 us)
Async XLA Ops:
  1.3 1.2 copy-start.14
  2.5 0.7 copy-start.19
  3.2 10.0 %copy-start.15 = (bf16[1,384,1280]{2,1,0:T(8,128)(2,1)S(1)}, bf16[1,384,1280]{2,1,0:T(8,128)(2,1)}, u32[]{:S(2)}) copy-start(bf16[1,384,1280]{2,1,0:T(8,128)(2,1)} %param.8) | copy-start | bytes 2949124
  5.4 22.9 %all-to-all-start = ((bf16[16,24,1280]{2,1,0:T(8,128)(2,1)}), bf16[16,24,1280]{2,1,0:T(8,128)(2,1)S(1)}, u32[]{:S(2)}, u32[]{:S(2)}) async-start(bf16[16,24,1280]{2,1,0:T(8,128)(2,1)} %bitcast.7), calls=%async_computation | async-start | bytes 1966080 | tf_op jit(solution)/shard_map/all_to_all | solution.py:256
  28.3 37.2 %copy-start.4 = (bf16[16,24,1280]{2,1,0:T(8,128)(2,1)}, bf16[16,24,1280]{2,1,0:T(8,128)(2,1)S(1)}, u32[]{:S(2)}) copy-start(bf16[16,24,1280]{2,1,0:T(8,128)(2,1)S(1)} %all-to-all-done) | copy-start | bytes 2949124
  28.3 31.6 %copy-start.1 = (bf16[1,1,5120,384]{3,2,1,0:T(8,128)(2,1)S(1)}, bf16[1,1,5120,384]{3,2,1,0:T(8,128)(2,1)}, u32[]{:S(2)}) copy-start(bf16[1,1,5120,384]{3,2,1,0:T(8,128)(2,1)} %param.11) | copy-start | bytes 11796484
  28.3 22.7 %collective-permute-start.1 = (bf16[384,1280]{1,0:T(8,128)(2,1)S(1)}, bf16[384,1280]{1,0:T(8,128)(2,1)S(1)}, u32[]{:S(2)}, u32[]{:S(2)}) collective-permute-start(bf16[384,1280]{1,0:T(8,128)(2,1)S(1)} %bitcast.33), channel_id=1, source_target_pairs={{0,3},{1,0},{2,1},{3,2},{4,7},{5,4},{6,5},{7,6},{8,11},{9,8},{10,9... | collective-permute-start | bytes 2949128 | tf_op jit(solution)/shard_map/ppermute | solution.py:16
  30.8 23.3 %collective-permute-start = (bf16[384,1280]{1,0:T(8,128)(2,1)S(1)}, bf16[384,1280]{1,0:T(8,128)(2,1)S(1)}, u32[]{:S(2)}, u32[]{:S(2)}) collective-permute-start(bf16[384,1280]{1,0:T(8,128)(2,1)S(1)} %bitcast.34), channel_id=1, source_target_pairs={{0,1},{1,2},{2,3},{3,0},{4,5},{5,6},{6,7},{7,4},{8,9},{9,10},{10,1... | collective-permute-start | bytes 2949128 | tf_op jit(solution)/shard_map/ppermute | solution.py:16
  49.2 29.4 %copy-start.5 = (bf16[16,24,1280]{2,1,0:T(8,128)(2,1)}, bf16[16,24,1280]{2,1,0:T(8,128)(2,1)S(1)}, u32[]{:S(2)}) copy-start(bf16[16,24,1280]{2,1,0:T(8,128)(2,1)S(1)} %all_to_all.15) | copy-start | bytes 2949124
  51.0 14.6 %copy-start.10 = (bf16[384,1280]{1,0:T(8,128)(2,1)}, bf16[384,1280]{1,0:T(8,128)(2,1)S(1)}, u32[]{:S(2)}) copy-start(bf16[384,1280]{1,0:T(8,128)(2,1)S(1)} %collective-permute-done.1.refs_4_.refs_2_) | copy-start | bytes 2949124
  54.1 11.5 %copy-start.11 = (bf16[384,1280]{1,0:T(8,128)(2,1)}, bf16[384,1280]{1,0:T(8,128)(2,1)S(1)}, u32[]{:S(2)}) copy-start(bf16[384,1280]{1,0:T(8,128)(2,1)S(1)} %collective-permute-done.refs_3_.refs_1_) | copy-start | bytes 2949124
  54.1 21.2 %collective-permute-start.3 = (bf16[384,1280]{1,0:T(8,128)(2,1)S(1)}, bf16[384,1280]{1,0:T(8,128)(2,1)S(1)}, u32[]{:S(2)}, u32[]{:S(2)}) collective-permute-start(bf16[384,1280]{1,0:T(8,128)(2,1)S(1)} %bitcast.37), channel_id=1, source_target_pairs={{0,3},{1,0},{2,1},{3,2},{4,7},{5,4},{6,5},{7,6},{8,11},{9,8},{10,9... | collective-permute-start | bytes 2949128 | tf_op jit(solution)/shard_map/ppermute | solution.py:16
  54.5 22.4 %collective-permute-start.2 = (bf16[384,1280]{1,0:T(8,128)(2,1)S(1)}, bf16[384,1280]{1,0:T(8,128)(2,1)S(1)}, u32[]{:S(2)}, u32[]{:S(2)}) collective-permute-start(bf16[384,1280]{1,0:T(8,128)(2,1)S(1)} %bitcast.38), channel_id=1, source_target_pairs={{0,1},{1,2},{2,3},{3,0},{4,5},{5,6},{6,7},{7,4},{8,9},{9,10},{10,1... | collective-permute-start | bytes 2949128 | tf_op jit(solution)/shard_map/ppermute | solution.py:16
  55.6 4.4 %collective-permute-start.4 = (s32[6,384]{1,0:T(8,128)S(1)}, s32[6,384]{1,0:T(8,128)S(1)}, u32[]{:S(2)}, u32[]{:S(2)}) collective-permute-start(s32[6,384]{1,0:T(8,128)S(1)} %bitcast.44), channel_id=1, source_target_pairs={{0,64},{64,0},{1,65},{65,1},{2,66},{66,2},{3,67},{67,3},{4,68},{68... | collective-permute-start | bytes 27656 | tf_op jit(solution)/shard_map/ppermute | solution.py:16
  58.3 27.5 %collective-permute-start.6 = (bf16[384,640]{1,0:T(8,128)(2,1)S(1)}, bf16[384,640]{1,0:T(8,128)(2,1)S(1)}, u32[]{:S(2)}, u32[]{:S(2)}) collective-permute-start(bf16[384,640]{1,0:T(8,128)(2,1)S(1)} %slice.13), channel_id=1, source_target_pairs={{0,3},{1,0},{2,1},{3,2},{4,7},{5,4},{6,5},{7,6},{8,11},{9,8},{10,9... | collective-permute-start | bytes 1474568 | tf_op jit(solution)/shard_map/ppermute | solution.py:16
  60.0 27.5 %collective-permute-start.5 = (bf16[384,640]{1,0:T(8,128)(2,1)S(1)}, bf16[384,640]{1,0:T(8,128)(2,1)S(1)}, u32[]{:S(2)}, u32[]{:S(2)}) collective-permute-start(bf16[384,640]{1,0:T(8,128)(2,1)S(1)} %slice.12), channel_id=1, source_target_pairs={{0,1},{1,2},{2,3},{3,0},{4,5},{5,6},{6,7},{7,4},{8,9},{9,10},{10,1... | collective-permute-start | bytes 1474568 | tf_op jit(solution)/shard_map/ppermute | solution.py:16
  60.0 2.1 %copy-start.2 = (bf16[1,1,5120,384]{3,2,1,0:T(8,128)(2,1)S(1)}, bf16[1,1,5120,384]{3,2,1,0:T(8,128)(2,1)}, u32[]{:S(2)}) copy-start(bf16[1,1,5120,384]{3,2,1,0:T(8,128)(2,1)} %param.12) | copy-start | bytes 11796484
  62.1 16.5 %copy-start = (bf16[1,1,384,5120]{3,2,1,0:T(8,128)(2,1)S(1)}, bf16[1,1,384,5120]{3,2,1,0:T(8,128)(2,1)}, u32[]{:S(2)}) copy-start(bf16[1,1,384,5120]{3,2,1,0:T(8,128)(2,1)} %param.13) | copy-start | bytes 11796484
  65.6 12.9 %copy-start.20 = (bf16[384,384]{1,0:T(8,128)(2,1)}, bf16[384,384]{1,0:T(8,128)(2,1)S(1)}, u32[]{:S(2)}) copy-start(bf16[384,384]{1,0:T(8,128)(2,1)S(1)} %get-tuple-element.55.choice_ref) | copy-start | bytes 884740
  75.3 5.0 %copy-start.12 = (bf16[384,1280]{1,0:T(8,128)(2,1)}, bf16[384,1280]{1,0:T(8,128)(2,1)S(1)}, u32[]{:S(2)}) copy-start(bf16[384,1280]{1,0:T(8,128)(2,1)S(1)} %collective-permute-done.3.y2.refs_7_) | copy-start | bytes 2949124
  76.9 3.4 %copy-start.13 = (bf16[384,1280]{1,0:T(8,128)(2,1)}, bf16[384,1280]{1,0:T(8,128)(2,1)S(1)}, u32[]{:S(2)}) copy-start(bf16[384,1280]{1,0:T(8,128)(2,1)S(1)} %collective-permute-done.2.y1.refs_6_) | copy-start | bytes 2949124
  77.0 19.4 %collective-permute-start.8 = (bf16[384,640]{1,0:T(8,128)(2,1)S(1)}, bf16[384,640]{1,0:T(8,128)(2,1)S(1)}, u32[]{:S(2)}, u32[]{:S(2)}) collective-permute-start(bf16[384,640]{1,0:T(8,128)(2,1)S(1)} %slice.15), channel_id=1, source_target_pairs={{0,3},{1,0},{2,1},{3,2},{4,7},{5,4},{6,5},{7,6},{8,11},{9,8},{10,9... | collective-permute-start | bytes 1474568 | tf_op jit(solution)/shard_map/ppermute | solution.py:16
  77.4 20.6 %collective-permute-start.7 = (bf16[384,640]{1,0:T(8,128)(2,1)S(1)}, bf16[384,640]{1,0:T(8,128)(2,1)S(1)}, u32[]{:S(2)}, u32[]{:S(2)}) collective-permute-start(bf16[384,640]{1,0:T(8,128)(2,1)S(1)} %slice.14), channel_id=1, source_target_pairs={{0,1},{1,2},{2,3},{3,0},{4,5},{5,6},{6,7},{7,4},{8,9},{9,10},{10,1... | collective-permute-start | bytes 1474568 | tf_op jit(solution)/shard_map/ppermute | solution.py:16
  78.5 19.4 %copy-start.3 = (bf16[1,1,5120,384]{3,2,1,0:T(8,128)(2,1)S(1)}, bf16[1,1,5120,384]{3,2,1,0:T(8,128)(2,1)}, u32[]{:S(2)}) copy-start(bf16[1,1,5120,384]{3,2,1,0:T(8,128)(2,1)} %param.12) | copy-start | bytes 11796484
  85.8 15.5 %copy-start.6 = (bf16[384,640]{1,0:T(8,128)(2,1)}, bf16[384,640]{1,0:T(8,128)(2,1)S(1)}, u32[]{:S(2)}) copy-start(bf16[384,640]{1,0:T(8,128)(2,1)S(1)} %collective-permute-done.6.x31.refs_4_) | copy-start | bytes 1474564
  87.4 13.9 %copy-start.7 = (bf16[384,640]{1,0:T(8,128)(2,1)}, bf16[384,640]{1,0:T(8,128)(2,1)S(1)}, u32[]{:S(2)}) copy-start(bf16[384,640]{1,0:T(8,128)(2,1)S(1)} %collective-permute-done.5.x30.refs_3_) | copy-start | bytes 1474564
  96.4 5.0 %copy-start.8 = (bf16[384,640]{1,0:T(8,128)(2,1)}, bf16[384,640]{1,0:T(8,128)(2,1)S(1)}, u32[]{:S(2)}) copy-start(bf16[384,640]{1,0:T(8,128)(2,1)S(1)} %collective-permute-done.8.y31.refs_9_) | copy-start | bytes 1474564
  98.0 3.4 %copy-start.9 = (bf16[384,640]{1,0:T(8,128)(2,1)}, bf16[384,640]{1,0:T(8,128)(2,1)S(1)}, u32[]{:S(2)}) copy-start(bf16[384,640]{1,0:T(8,128)(2,1)S(1)} %collective-permute-done.7.y30.refs_8_) | copy-start | bytes 1474564
  101.4 0.7 copy-start.18
  102.1 5.9 %copy-start.16 = (bf16[384,384]{1,0:T(8,128)(2,1)}, bf16[384,384]{1,0:T(8,128)(2,1)S(1)}, u32[]{:S(2)}) copy-start(bf16[384,384]{1,0:T(8,128)(2,1)S(1)} %get-tuple-element.74.dg_ref.refs_10_) | copy-start | bytes 884740
  102.1 5.9 %copy-start.17 = (bf16[384,384]{1,0:T(8,128)(2,1)}, bf16[384,384]{1,0:T(8,128)(2,1)S(1)}, u32[]{:S(2)}) copy-start(bf16[384,384]{1,0:T(8,128)(2,1)S(1)} %get-tuple-element.75.du_ref.refs_11_) | copy-start | bytes 884740
  102.1 11.0 %collective-permute-start.9 = (bf16[384,640]{1,0:T(8,128)(2,1)S(1)}, bf16[384,640]{1,0:T(8,128)(2,1)S(1)}, u32[]{:S(2)}, u32[]{:S(2)}) collective-permute-start(bf16[384,640]{1,0:T(8,128)(2,1)S(1)} %get-tuple-element.64), channel_id=1, source_target_pairs={{0,1},{1,2},{2,3},{3,0},{4,5},{5,6},{6,7},{7,4},{8,9},{9,10},{10,1... | collective-permute-start | bytes 1474568 | tf_op jit(solution)/shard_map/ppermute | solution.py:16
  102.1 11.2 %collective-permute-start.12 = (bf16[384,640]{1,0:T(8,128)(2,1)S(1)}, bf16[384,640]{1,0:T(8,128)(2,1)S(1)}, u32[]{:S(2)}, u32[]{:S(2)}) collective-permute-start(bf16[384,640]{1,0:T(8,128)(2,1)S(1)} %get-tuple-element.68), channel_id=1, source_target_pairs={{0,3},{1,0},{2,1},{3,2},{4,7},{5,4},{6,5},{7,6},{8,11},{9,8},{10,9... | collective-permute-start | bytes 1474568 | tf_op jit(solution)/shard_map/ppermute | solution.py:16
  108.0 14.5 %collective-permute-start.11 = (bf16[384,640]{1,0:T(8,128)(2,1)S(1)}, bf16[384,640]{1,0:T(8,128)(2,1)S(1)}, u32[]{:S(2)}, u32[]{:S(2)}) collective-permute-start(bf16[384,640]{1,0:T(8,128)(2,1)S(1)} %get-tuple-element.65), channel_id=1, source_target_pairs={{0,3},{1,0},{2,1},{3,2},{4,7},{5,4},{6,5},{7,6},{8,11},{9,8},{10,9... | collective-permute-start | bytes 1474568 | tf_op jit(solution)/shard_map/ppermute | solution.py:16
  113.2 10.1 %collective-permute-start.10 = (bf16[384,640]{1,0:T(8,128)(2,1)S(1)}, bf16[384,640]{1,0:T(8,128)(2,1)S(1)}, u32[]{:S(2)}, u32[]{:S(2)}) collective-permute-start(bf16[384,640]{1,0:T(8,128)(2,1)S(1)} %add_convert_fusion.1), channel_id=1, source_target_pairs={{0,1},{1,2},{2,3},{3,0},{4,5},{5,6},{6,7},{7,4},{8,9},{9,10},{10,1... | collective-permute-start | bytes 1474568 | tf_op jit(solution)/shard_map/ppermute | solution.py:16
  123.5 9.5 %collective-permute-start.13 = (bf16[384,640]{1,0:T(8,128)(2,1)S(1)}, bf16[384,640]{1,0:T(8,128)(2,1)S(1)}, u32[]{:S(2)}, u32[]{:S(2)}) collective-permute-start(bf16[384,640]{1,0:T(8,128)(2,1)S(1)} %get-tuple-element.69), channel_id=1, source_target_pairs={{0,1},{1,2},{2,3},{3,0},{4,5},{5,6},{6,7},{7,4},{8,9},{9,10},{10,1... | collective-permute-start | bytes 1474568 | tf_op jit(solution)/shard_map/ppermute | solution.py:16
  123.5 9.4 %collective-permute-start.14 = (bf16[384,640]{1,0:T(8,128)(2,1)S(1)}, bf16[384,640]{1,0:T(8,128)(2,1)S(1)}, u32[]{:S(2)}, u32[]{:S(2)}) collective-permute-start(bf16[384,640]{1,0:T(8,128)(2,1)S(1)} %add_convert_fusion), channel_id=1, source_target_pairs={{0,3},{1,0},{2,1},{3,2},{4,7},{5,4},{6,5},{7,6},{8,11},{9,8},{10,9... | collective-permute-start | bytes 1474568 | tf_op jit(solution)/shard_map/ppermute | solution.py:16
  126.3 9.2 %collective-permute-start.15 = (bf16[384,640]{1,0:T(8,128)(2,1)S(1)}, bf16[384,640]{1,0:T(8,128)(2,1)S(1)}, u32[]{:S(2)}, u32[]{:S(2)}) collective-permute-start(bf16[384,640]{1,0:T(8,128)(2,1)S(1)} %shard_map.108), channel_id=1, source_target_pairs={{0,64},{64,0},{1,65},{65,1},{2,66},{66,2},{3,67},{67,3},{4,68},{68... | collective-permute-start | bytes 1474568 | tf_op jit(solution)/shard_map/ppermute | solution.py:16
  136.7 30.8 %all-to-all-start.2 = ((bf16[32,24,640]{2,1,0:T(8,128)(2,1)}), bf16[32,24,640]{2,1,0:T(8,128)(2,1)S(1)}, u32[]{:S(2)}, u32[]{:S(2)}) async-start(bf16[32,24,640]{2,1,0:T(8,128)(2,1)} %bitcast.14), calls=%async_computation.2 | async-start | bytes 1966080 | tf_op jit(solution)/shard_map/all_to_all | solution.py:347
  151.4 16.2 %copy-start.21 = (bf16[384,384]{1,0:T(8,128)(2,1)S(1)}, bf16[384,384]{1,0:T(8,128)(2,1)}, u32[]{:S(2)}) copy-start(bf16[384,384]{1,0:T(8,128)(2,1)} %copy-done.20) | copy-start | bytes 884740
